TPU v7x, 128 devices: a whole 4x4x4 slice. The times are simulated.
128 devices in a mesh: ctx: 8 (over z, y_hi), tp: 16 (over y_lo, x, core).
Axes of the slice: x: 4, y: 4 (y_hi: 2, y_lo: 2; y = y_hi * 2 + y_lo), z: 4, core: 2. Of those that a mesh axis runs over, the one named last changes fastest.
Arguments:
- queries: bfloat16 [4096, 12288], P('ctx', 'tp'), may hold values from -10 to 10
- kv_latent: bfloat16 [4096, 512], P(('ctx', 'tp')), may hold values from -6 to 6
- key_rope: bfloat16 [4096, 64], P(('ctx', 'tp')), may hold values from -6 to 6
- w_key: bfloat16 [512, 8192], P(None, 'tp'), may hold values from -0.25 to 0.25
- w_value: bfloat16 [512, 8192], P(None, 'tp'), may hold values from -0.25 to 0.25
- w_out: bfloat16 [8192, 2560], P('tp'), may hold values from -0.25 to 0.25
- residual: bfloat16 [4096, 2560], P(('ctx', 'tp')), may hold values from -36 to 36
- moe_gain: float32 [2560], replicated, may hold values from 0.5 to 1.5
- shared_gate: bfloat16 [2560, 3072], P(None, 'tp'), may hold values from -0.125 to 0.125
- shared_up: bfloat16 [2560, 3072], P(None, 'tp'), may hold values from -0.125 to 0.125
- shared_down: bfloat16 [3072, 2560], P('tp'), may hold values from -0.109375 to 0.109375
- expert_gate_up: bfloat16 [128, 2560, 1536], P(('ctx', 'tp')), may hold values from -0.125 to 0.125
- expert_down: bfloat16 [128, 768, 2560], P(('ctx', 'tp')), may hold values from -0.21875 to 0.21875
- expert_ids: int32 [4096, 6], P(('ctx', 'tp')), may hold values from 0 to 127, all different within a row; in each aligned block of 32 rows (0 to 31, 32 to 63, ...) at most 3 rows name the same one
- gate_weights: float32 [4096, 6], P(('ctx', 'tp')), may hold values from 0.1 to 0.6
Outputs:
- layer_out: bfloat16 [4096, 2560], P(('ctx', 'tp'))
Inputs may be any that keep to these rules, and one draw needn't show every extreme that they name: `expert_ids`: each row names 6 different experts; among the rows that one device holds no expert is named more than 3 times, and on some device one expert is named exactly 3 times; every expert is named somewhere.
All inputs are finite; a program needn't handle non-finite values.
Results may differ from a plain program's by a relative error of at most 0.022.
Values may be sent and summed in bfloat16 or wider, within the bound.
A program may use at most 128 MiB of HBM per device.

v0:
```python
import math

import jax
import jax.numpy as jnp
from jax import lax
from jax.sharding import PartitionSpec as P

NOPE = 128
ROPE = 64
VDIM = 128
TOPK = 6


masked_score = -1e30


def attend_block(
    carry_state, query_nope, query_rope, query_position, key_nope, values, key_rows, key_position
):
    top_old, total_old, weighted = carry_state
    head_count = query_nope.shape[1]
    key_heads = key_nope.reshape(key_nope.shape[0], head_count, NOPE)
    value_heads = values.reshape(values.shape[0], head_count, VDIM)
    scores = jnp.einsum("shd,rhd->shr", query_nope, key_heads, preferred_element_type=jnp.float32)
    scores = scores + jnp.einsum(
        "shd,rd->shr", query_rope, key_rows, preferred_element_type=jnp.float32
    )
    scores = scores * (1.0 / math.sqrt(NOPE + ROPE))
    visible = (key_position[None, :] <= query_position[:, None])[:, None, :]
    top_new = jnp.maximum(top_old, jnp.max(jnp.where(visible, scores, masked_score), axis=2))
    weights = jnp.where(visible, jnp.exp(scores - top_new[:, :, None]), 0.0)
    factor = jnp.exp(top_old - top_new)
    total_new = total_old * factor + jnp.sum(weights, axis=2)
    update = jnp.einsum(
        "shr,rhd->shd",
        weights.astype(jnp.bfloat16),
        value_heads,
        preferred_element_type=jnp.float32,
    )
    weighted = weighted * factor[:, :, None] + update
    return (top_new, total_new, weighted)


def sweep_keys(carry_state, query_parts, key_nope, values, key_rows):
    query_nope, query_rope, query_position = query_parts
    row_total = key_nope.shape[0]
    block_rows = math.gcd(row_total, 512)

    def advance(turn_index, partial_value):
        offset = turn_index * block_rows
        return attend_block(
            partial_value,
            query_nope,
            query_rope,
            query_position,
            lax.dynamic_slice_in_dim(key_nope, offset, block_rows, 0),
            lax.dynamic_slice_in_dim(values, offset, block_rows, 0),
            lax.dynamic_slice_in_dim(key_rows, offset, block_rows, 0),
            offset + jnp.arange(block_rows, dtype=jnp.int32),
        )

    return lax.fori_loop(0, row_total // block_rows, advance, carry_state)


def keep_state(partial_value):
    return partial_value


def shards(
    queries,
    kv_latent,
    key_rope,
    w_key,
    w_value,
    w_out,
    residual,
    moe_gain,
    shared_gate,
    shared_up,
    shared_down,
    expert_gate_up,
    expert_down,
    expert_ids,
    gate_weights,
):
    seq_rows = queries.shape[0]
    token_rows = residual.shape[0]
    model_width = residual.shape[1]
    head_count = w_key.shape[1] // NOPE
    query_heads = queries.reshape(seq_rows, head_count, NOPE + ROPE)
    first_query = lax.axis_index("ctx") * seq_rows
    query_position = first_query + jnp.arange(seq_rows, dtype=jnp.int32)
    last_query = first_query + seq_rows - 1
    query_parts = (query_heads[:, :, :NOPE], query_heads[:, :, NOPE:], query_position)
    initial = (
        jnp.full((seq_rows, head_count), masked_score, jnp.float32),
        jnp.zeros((seq_rows, head_count), jnp.float32),
        jnp.zeros((seq_rows, head_count, VDIM), jnp.float32),
    )
    shard_latent, shard_rope = (
        lax.all_gather(kv_latent, "tp", axis=0, tiled=True),
        lax.all_gather(key_rope, "tp", axis=0, tiled=True),
    )
    pieces = (
        lax.all_gather(shard_latent, "ctx", axis=0, tiled=True),
        lax.all_gather(shard_rope, "ctx", axis=0, tiled=True),
    )

    def attend_piece(inner):
        key_nope = jnp.dot(pieces[0], w_key, preferred_element_type=jnp.float32).astype(
            jnp.bfloat16
        )
        values = jnp.dot(pieces[0], w_value, preferred_element_type=jnp.float32).astype(
            jnp.bfloat16
        )
        return sweep_keys(inner, query_parts, key_nope, values, pieces[1])

    final_state = lax.cond(jnp.int32(0) <= last_query, attend_piece, keep_state, initial)
    attention = (final_state[2] / final_state[1][:, :, None]).astype(jnp.bfloat16)
    attention = attention.reshape(seq_rows, head_count * VDIM)
    hidden_state = residual.astype(jnp.float32) + lax.psum_scatter(
        jnp.dot(attention, w_out, preferred_element_type=jnp.float32).astype(jnp.bfloat16),
        "tp",
        scatter_dimension=0,
        tiled=True,
    ).astype(jnp.float32)
    mean_square = jnp.mean(hidden_state * hidden_state, axis=1, keepdims=True)
    normed = (hidden_state * lax.rsqrt(mean_square + 1e-06) * moe_gain).astype(jnp.bfloat16)
    normed_block = lax.all_gather(normed, "tp", axis=0, tiled=True)
    gate_part = jnp.dot(normed_block, shared_gate, preferred_element_type=jnp.float32)
    up_part = jnp.dot(normed_block, shared_up, preferred_element_type=jnp.float32)
    shared_hidden = (jax.nn.silu(gate_part) * up_part).astype(jnp.bfloat16)
    shared_output = lax.psum_scatter(
        jnp.dot(shared_hidden, shared_down, preferred_element_type=jnp.float32).astype(
            jnp.bfloat16
        ),
        "tp",
        scatter_dimension=0,
        tiled=True,
    ).astype(jnp.float32)
    ctx_count = lax.axis_size("ctx")
    tp_count = lax.axis_size("tp")
    experts = ctx_count * tp_count
    capacity = (token_rows * TOPK + experts - 1) // experts + 1
    flat_experts = expert_ids.reshape(-1)
    onehot = (flat_experts[:, None] == jnp.arange(experts, dtype=jnp.int32)[None, :]).astype(
        jnp.int32
    )
    earlier = jnp.cumsum(onehot, axis=0) - onehot
    slot_index = jnp.sum(earlier * onehot, axis=1)
    targets = (flat_experts * capacity + slot_index).reshape(token_rows, TOPK)
    places = jnp.arange(experts * capacity, dtype=jnp.int32)
    placing = jnp.sum((places[:, None, None] == targets[None, :, :]).astype(jnp.bfloat16), axis=2)
    outgoing = jnp.dot(placing, normed, preferred_element_type=jnp.float32).astype(jnp.bfloat16)
    outgoing = outgoing.reshape(experts, capacity, model_width)
    received = lax.all_to_all(outgoing, ("ctx", "tp"), split_axis=0, concat_axis=0, tiled=True)
    item_shape = received.shape
    slot_rows = received.reshape(-1, item_shape[-1])
    half_width = expert_down.shape[1]
    gate_up_part = jnp.dot(slot_rows, expert_gate_up[0], preferred_element_type=jnp.float32)
    expert_hidden = (
        jax.nn.silu(gate_up_part[:, :half_width]) * gate_up_part[:, half_width:]
    ).astype(jnp.bfloat16)
    expert_output = jnp.dot(
        expert_hidden, expert_down[0], preferred_element_type=jnp.float32
    ).astype(jnp.bfloat16)
    returned = lax.all_to_all(
        expert_output.reshape(item_shape), ("ctx", "tp"), split_axis=0, concat_axis=0, tiled=True
    )
    picked = returned.reshape(experts * capacity, model_width)[targets.reshape(-1)]
    picked = picked.reshape(token_rows, TOPK, model_width)
    routed = jnp.einsum("tk,tkd->td", gate_weights, picked.astype(jnp.float32))
    return (hidden_state + shared_output + routed).astype(jnp.bfloat16)


def solution(mesh):
    in_specs = (
        P("ctx", "tp"),
        P(("ctx", "tp"), None),
        P(("ctx", "tp"), None),
        P(None, "tp"),
        P(None, "tp"),
        P("tp", None),
        P(("ctx", "tp"), None),
        P(),
        P(None, "tp"),
        P(None, "tp"),
        P("tp", None),
        P(("ctx", "tp"), None, None),
        P(("ctx", "tp"), None, None),
        P(("ctx", "tp"), None),
        P(("ctx", "tp"), None),
    )
    out_specs = P(("ctx", "tp"), None)
    return jax.shard_map(shards, mesh=mesh, in_specs=in_specs, out_specs=out_specs, check_vma=False)
```

profile of v0, /device:TPU:16, one launch (start us, length us, event | category | flops | bytes accessed | tf_op | source)
XLA Modules:
  0.0 507.3 jit_solution(1402923303150677932)
XLA Ops:
  6.5 22.6 %all_gather.15 = bf16[512,512]{1,0:T(8,128)(2,1)} all-gather(bf16[32,512]{1,0:T(8,128)(2,1)} %param.20), channel_id=1, replica_groups=mesh['ctx'=8,'tp'=16] {'tp'}, dimensions={0}, use_global_device_ids=true | all-gather | bytes 557056 | tf_op jit(solution)/shard_map/all_gather | solution.py:101
  29.2 17.0 %all_gather.17 = bf16[512,64]{1,0:T(8,128)(2,1)S(1)} all-gather(bf16[32,64]{1,0:T(8,128)(2,1)} %param.21), channel_id=1, replica_groups=mesh['ctx'=8,'tp'=16] {'tp'}, dimensions={0}, use_global_device_ids=true | all-gather | bytes 69632 | tf_op jit(solution)/shard_map/all_gather | solution.py:102
  46.2 46.9 %all_gather.18 = bf16[4096,64]{1,0:T(8,128)(2,1)} all-gather(bf16[512,64]{1,0:T(8,128)(2,1)S(1)} %all_gather.17), channel_id=1, replica_groups=mesh['ctx'=8,'tp'=16] {'ctx'}, dimensions={0}, use_global_device_ids=true | all-gather | bytes 589824 | tf_op jit(solution)/shard_map/all_gather | solution.py:106
  93.1 16.1 %all-gather.3.cloned.1.call-done = bf16[4096,512]{1,0:T(8,128)(2,1)} async-done(((bf16[512,512]{1,0:T(8,128)(2,1)}), bf16[4096,512]{1,0:T(8,128)(2,1)}) %all-gather.3.cloned.1.call-update) | async-done | bytes 4194320 | tf_op jit(solution)/shard_map/all_gather | solution.py:105
  109.2 173.4 %conditional.1 = (f32[512,4]{0,1:T(4,128)}, f32[512,4,128]{0,2,1:T(8,128)}) conditional(s32[]{:T(128)} %convert_element_type.65, () %tuple.31, (bf16[4096,512]{1,0:T(8,128)(2,1)}, bf16[512,512]{1,0:T(8,128)(2,1)}, bf16[512,512]{1,0:T(8,128)(2,1)}, bf16[512,768]{1,0:T(8,128)(2,1)}, s32[]{:T(128)}, /*index=5*/s32[512]{0:T(512)S(1)}, ...), branch_computations={%region_0.0_spmd, %region_1.6_spmd} | conditional | flops 4981795840 | bytes 72296848 | solution.py:118
  109.2 6.7 %convolution_convert_fusion = bf16[4096,512]{1,0:T(8,128)(2,1)} fusion(bf16[4096,512]{1,0:T(8,128)(2,1)} %get-tuple-element.209, bf16[512,512]{1,0:T(8,128)(2,1)} %get-tuple-element.224), kind=kOutput, calls=%fused_computation.26 | convolution fusion | flops 2149580800 | bytes 8912896 | tf_op jit(solution)/shard_map/cond/branch_1_fun/dot_general | solution.py:113
  115.9 4.3 convolution_convert_fusion.1
  127.6 155.0 %while.20 = (s32[]{:T(128)}, f32[512,4]{0,1:T(4,128)S(1)}, f32[512,4]{0,1:T(4,128)}, f32[512,4,128]{0,2,1:T(8,128)}, s32[512]{0:T(512)S(1)}, /*index=5*/bf16[409...) while((s32[]{:T(128)}, f32[512,4]{0,1:T(4,128)S(1)}, ...), condition=%wide.region_5.5_spmd.clone, body=%wide.region_2.4_spmd.clone.sunk | while | flops 682633728 | bytes 30349512 | solution.py:62
  132.9 4.2 select_reduce_fusion.2
  137.1 3.0 fusion.80
  141.9 4.2 fusion.82
  151.4 4.2 select_reduce_fusion.2
  155.6 3.0 fusion.80
  161.1 4.5 fusion.82
  170.9 4.2 select_reduce_fusion.2
  175.1 3.0 fusion.80
  180.6 4.5 fusion.82
  190.4 4.2 select_reduce_fusion.2
  194.6 3.0 fusion.80
  200.1 4.5 fusion.82
  209.9 4.2 select_reduce_fusion.2
  214.1 3.0 fusion.80
  219.6 4.5 fusion.82
  229.4 4.2 select_reduce_fusion.2
  233.5 3.0 fusion.80
  239.1 4.5 fusion.82
  248.9 4.2 select_reduce_fusion.2
  253.0 3.0 fusion.80
  258.6 4.5 fusion.82
  268.4 4.2 select_reduce_fusion.2
  272.5 3.0 fusion.80
  278.1 4.5 fusion.82
  284.0 3.1 convolution_convert_fusion.3
  287.3 62.8 %reduce-scatter.3.cloned.1.call-done = bf16[32,2560]{1,0:T(8,128)(2,1)} async-done(((bf16[512,2560]{1,0:T(8,128)(2,1)}), bf16[32,2560]{1,0:T(8,128)(2,1)}) %reduce-scatter.3.cloned.1.call-update) | async-done | bytes 163856 | tf_op jit(solution)/shard_map/reduce_scatter | solution.py:121
  353.9 2.9 convolution_convert_fusion.5
  356.9 5.6 %reshape.128 = bf16[128,3,2560]{2,1,0:T(4,128)(2,1)} reshape(bf16[384,2560]{1,0:T(8,128)(2,1)} %convolution_convert_fusion.5) | data formatting | bytes 3932160 | tf_op jit(solution)/shard_map/reshape | solution.py:155
  362.4 7.4 %all-to-all-start = ((bf16[128,3,2560]{2,1,0:T(4,128)(2,1)}), bf16[128,3,2560]{2,1,0:T(4,128)(2,1)}, u32[]{:S(2)}, u32[]{:S(2)}) async-start(bf16[128,3,2560]{2,1,0:T(4,128)(2,1)} %reshape.128), calls=%async_computation.2 | async-start | bytes 5242880 | tf_op jit(solution)/shard_map/all_to_all | solution.py:156
  369.9 38.1 %all-gather.5.cloned.1.call-done = bf16[512,2560]{1,0:T(8,128)(2,1)} async-done(((bf16[32,2560]{1,0:T(8,128)(2,1)}), bf16[512,2560]{1,0:T(8,128)(2,1)}) %all-gather.5.cloned.1.call-update) | async-done | bytes 2621456 | tf_op jit(solution)/shard_map/all_gather | solution.py:129
  407.9 3.0 fusion.43
  410.9 5.7 %convolution_convert_fusion.2 = bf16[512,2560]{1,0:T(8,128)(2,1)} fusion(bf16[192,2560]{1,0:T(8,128)(2,1)} %param.29, bf16[512,2560]{1,0:T(8,128)(2,1)} %all-gather.5.cloned.1.call-done, bf16[2560,192]{0,1:T(8,128)(2,1)} %param.28, f32[512,192]{0,1:T(8,128)S(1)} %fusion.43), kind=kOutput, calls=%fused_computation.31 | convolution fusion | flops 1008533504 | bytes 7602176 | tf_op jit(solution)/shard_map/dot_general | solution.py:134
  416.6 5.4 %reshape.129 = bf16[384,2560]{1,0:T(8,128)(2,1)} reshape(bf16[128,3,2560]{2,1,0:T(4,128)(2,1)} %all-to-all-done) | data formatting | bytes 3932160 | tf_op jit(solution)/shard_map/reshape | solution.py:158
  422.0 6.3 %fusion.19 = f32[384,1536]{1,0:T(8,128)S(1)} fusion(bf16[384,2560]{1,0:T(8,128)(2,1)} %reshape.129, bf16[1,2560,1536]{2,1,0:T(8,128)(2,1)} %param.30), kind=kOutput, calls=%fused_computation.29 | convolution fusion | flops 3019898880 | bytes 12189696 | tf_op jit(solution)/shard_map/dot_general | solution.py:160
  428.3 3.0 convolution_convert_fusion.4
  431.3 5.5 %reshape.130 = bf16[128,3,2560]{2,1,0:T(4,128)(2,1)} reshape(bf16[384,2560]{1,0:T(8,128)(2,1)} %convolution_convert_fusion.4) | data formatting | bytes 3932160 | tf_op jit(solution)/shard_map/reshape | solution.py:168
  436.8 8.9 %all-to-all-start.1 = ((bf16[128,3,2560]{2,1,0:T(4,128)(2,1)}), bf16[128,3,2560]{2,1,0:T(4,128)(2,1)}, u32[]{:S(2)}, u32[]{:S(2)}) async-start(bf16[128,3,2560]{2,1,0:T(4,128)(2,1)} %reshape.130), calls=%async_computation.3 | async-start | bytes 5242880 | tf_op jit(solution)/shard_map/all_to_all | solution.py:167
  446.0 38.7 %all-to-all-done.1 = bf16[128,3,2560]{2,1,0:T(4,128)(2,1)} async-done(((bf16[128,3,2560]{2,1,0:T(4,128)(2,1)}), bf16[128,3,2560]{2,1,0:T(4,128)(2,1)}, u32[]{:S(2)}, u32[]{:S(2)}) %all-to-all-start.1) | async-done | bytes 1966112 | tf_op jit(solution)/shard_map/all_to_all | solution.py:167
  484.6 5.4 %reshape.131 = bf16[384,2560]{1,0:T(8,128)(2,1)} reshape(bf16[128,3,2560]{2,1,0:T(4,128)(2,1)} %all-to-all-done.1) | data formatting | bytes 3932160 | tf_op jit(solution)/shard_map/reshape | solution.py:170
  490.0 5.0 gather_fusion
  (137 shorter events, 80.8 us)
Async XLA Ops:
  6.5 277.4 %copy-start = (bf16[512,2560]{1,0:T(8,128)(2,1)S(1)}, bf16[512,2560]{1,0:T(8,128)(2,1)}, u32[]{:S(2)}) copy-start(bf16[512,2560]{1,0:T(8,128)(2,1)} %param.24) | copy-start | bytes 7864324
  6.5 102.6 %all-gather.3.cloned.1.call-start = ((), (), s32[]{:S(2)}) async-start(), calls=%async_computation.4 | async-start | bytes 4718592 | tf_op jit(solution)/shard_map/all_gather | solution.py:105
  29.1 320.9 %reduce-scatter.3.cloned.1.call-start = ((), (), s32[]{:S(2)}) async-start(), calls=%async_computation.5 | async-start | bytes 2785280 | tf_op jit(solution)/shard_map/reduce_scatter | solution.py:121
  109.2 6.8 %copy-start.6 = (bf16[4096,512]{1,0:T(8,128)(2,1)S(1)}, bf16[4096,512]{1,0:T(8,128)(2,1)}, u32[]{:S(2)}) copy-start(bf16[4096,512]{1,0:T(8,128)(2,1)} %get-tuple-element.209) | copy-start | bytes 12582916 | tf_op jit(solution)/shard_map/cond
  109.2 6.8 %copy-start.8 = (bf16[512,512]{1,0:T(8,128)(2,1)S(1)}, bf16[512,512]{1,0:T(8,128)(2,1)}, u32[]{:S(2)}) copy-start(bf16[512,512]{1,0:T(8,128)(2,1)} %get-tuple-element.223) | copy-start | bytes 1572868 | tf_op jit(solution)/shard_map/cond
  284.0 66.1 %copy-start.1 = (bf16[32,2560]{1,0:T(8,128)(2,1)S(1)}, bf16[32,2560]{1,0:T(8,128)(2,1)}, u32[]{:S(2)}) copy-start(bf16[32,2560]{1,0:T(8,128)(2,1)} %param.25) | copy-start | bytes 491524
  284.0 67.2 %copy-start.3 = (f32[2560]{0:T(1024)S(1)}, f32[2560]{0:T(1024)}, u32[]{:S(2)}) copy-start(f32[2560]{0:T(1024)} %param.26) | copy-start | bytes 30724
  284.0 68.9 %copy-start.4 = (s32[32,6]{0,1:T(8,128)S(1)}, s32[32,6]{0,1:T(8,128)}, u32[]{:S(2)}) copy-start(s32[32,6]{0,1:T(8,128)} %param.32) | copy-start | bytes 2308
  287.1 120.9 %all-gather.5.cloned.1.call-start = ((), (), s32[]{:S(2)}) async-start(), calls=%async_computation.6 | async-start | bytes 2785280 | tf_op jit(solution)/shard_map/all_gather | solution.py:129
  362.4 54.2 %all-to-all-start = ((bf16[128,3,2560]{2,1,0:T(4,128)(2,1)}), bf16[128,3,2560]{2,1,0:T(4,128)(2,1)}, u32[]{:S(2)}, u32[]{:S(2)}) async-start(bf16[128,3,2560]{2,1,0:T(4,128)(2,1)} %reshape.128), calls=%async_computation.2 | async-start | bytes 5242880 | tf_op jit(solution)/shard_map/all_to_all | solution.py:156
  369.8 129.3 %reduce-scatter.5.cloned.1.call-start = ((), (), s32[]{:S(2)}) async-start(), calls=%async_computation.7 | async-start | bytes 2785280 | tf_op jit(solution)/shard_map/reduce_scatter | solution.py:133
  422.0 6.3 %copy-start.7 = (bf16[1,768,2560]{2,1,0:T(8,128)(2,1)S(1)}, bf16[1,768,2560]{2,1,0:T(8,128)(2,1)}, u32[]{:S(2)}) copy-start(bf16[1,768,2560]{2,1,0:T(8,128)(2,1)} %param.31) | copy-start | bytes 11796484
  431.3 14.5 %copy-start.5 = (f32[32,6]{0,1:T(8,128)S(1)}, f32[32,6]{0,1:T(8,128)}, u32[]{:S(2)}) copy-start(f32[32,6]{0,1:T(8,128)} %param.33) | copy-start | bytes 2308
  436.8 47.8 %all-to-all-start.1 = ((bf16[128,3,2560]{2,1,0:T(4,128)(2,1)}), bf16[128,3,2560]{2,1,0:T(4,128)(2,1)}, u32[]{:S(2)}, u32[]{:S(2)}) async-start(bf16[128,3,2560]{2,1,0:T(4,128)(2,1)} %reshape.130), calls=%async_computation.3 | async-start | bytes 5242880 | tf_op jit(solution)/shard_map/all_to_all | solution.py:167
  495.0 4.1 copy-start.2
Sparse Core Ops, SparseCore 0:
  29.3 79.8 all-gather.2
  287.2 62.8 reduce-scatter.2
  353.0 54.8 all-gather.4
  416.7 74.7 reduce-scatter.4
where the time goes:
time: 514 us; the launch traced here: 507 us
  waiting for transfers between devices  156 us (30%)
  matrix products  122 us (24%)
  blocking collectives  86.5 us (17%)
  local copies, waits for them, and re-layouts  71.7 us (14%)
  other arithmetic  41.7 us (8%)
  starting transfers between devices  16.6 us (3%)
  between operations  13.3 us (3%)
    reduce_scatter x1, waiting for transfers between devices, shards(): lax.psum_scatter(jnp.dot(attention, w_out, preferred_element_type=jnp.flo...  62.8 us
    all_gather x1, blocking collectives, shards(): lax.all_gather(shard_rope, 'ctx', axis=0, tiled=True)  46.9 us
    all_to_all x1, waiting for transfers between devices, shards(): lax.all_to_all(expert_output.reshape(item_shape), ('ctx', 'tp'), split_ax...  38.7 us
    all_gather x1, waiting for transfers between devices, shards(): normed_block = lax.all_gather(normed, 'tp', axis=0, tiled=True)  38.1 us
    dot_general x8, matrix products, attend_block(): jnp.einsum('shr,rhd->shd', weights.astype(jnp.bfloat16), value_heads, pre...  35.8 us
    dot_general x8, matrix products, attend_block(): jnp.einsum('shd,rd->shr', query_rope, key_rows, preferred_element_type=jn...  33.3 us
    dynamic_slice x16, local copies, waits for them, and re-layouts, advance(): lax.dynamic_slice_in_dim(values, offset, block_rows, 0)  26.5 us
    reduce_sum x8, other arithmetic, attend_block(): total_new = total_old * factor + jnp.sum(weights, axis=2)  23.7 us
  transfers between devices with their start and end apart: 6, of which 4 were waited for; matrix products, arithmetic and copies ran while one was open for 10% of the time, Pallas kernels for 0%

commit v1 on v0

v1 whole, which is shorter than its diff:
```python
import functools
import math

import jax
import jax.numpy as jnp
from jax import lax
from jax.experimental import pallas as pl
from jax.experimental.pallas import tpu as pltpu
from jax.sharding import PartitionSpec as P

NOPE = 128
ROPE = 64
VDIM = 128
TOPK = 6
CAP = 3
MESH = pl.DeviceIdType.MESH
F32 = jnp.float32
BF16 = jnp.bfloat16
LOW = -1e30
CHUNKS = 5


def loop(first, end, body):
    def step(i, carry):
        body(i)
        return carry

    lax.fori_loop(first, end, step, 0)


def dot(a, b):
    return jnp.dot(a, b, preferred_element_type=F32)


def layer_kernel(
    tail_ref,
    queries,
    w_key,
    w_value,
    w_out_hbm,
    residual,
    gain,
    shared_gate_hbm,
    shared_up_hbm,
    shared_down_hbm,
    gate_up_hbm,
    down_hbm,
    out_ref,
    w_out,
    shared_gate,
    shared_up,
    shared_down,
    gate_up,
    down,
    load_sem,
    lat,
    q_s,
    k_s,
    v_s,
    top_s,
    acc_s,
    lat_ctx_send,
    lat_ctx_recv,
    lat_tp_send,
    lat_tp_recv,
    lat_sib_send,
    lat_sib_recv,
    part,
    sib_in,
    row_in,
    a_sib_send,
    a_sib_recv,
    a_row_send,
    a_row_recv,
    hidden,
    normed,
    n_send,
    n_recv,
    n_sib_send,
    n_sib_recv,
    pick,
    give,
    slots_out,
    slots_in,
    up_acc,
    x_send,
    x_recv,
    back_out,
    back_in,
    y_send,
    y_recv,
    shared_acc,
    part2,
    sib_in2,
    row_in2,
    b_sib_send,
    b_sib_recv,
    b_row_send,
    b_row_recv,
):
    c = lax.axis_index("ctx")
    t = lax.axis_index("tp")
    chip = t // 2
    core = t % 2
    other = 1 - core
    sibling = (c, chip * 2 + other)
    rows = residual.shape[0]
    width = residual.shape[1]
    heads = q_s.shape[0]
    latent = w_key.shape[0]
    n_ctx, _, n_chip = lat.shape[:3]
    half = n_chip * rows
    group = 2 * half
    span = width // CHUNKS
    slot_room = slots_out.shape[1]

    def cols(n):
        return pl.ds(n * span, span)

    def remote(src, dst, send, recv, device):
        return pltpu.make_async_remote_copy(
            src_ref=src,
            dst_ref=dst,
            send_sem=send,
            recv_sem=recv,
            device_id=device,
            device_id_type=MESH,
        )

    def chip_at(d):
        j = (chip + d) % n_chip
        return j, (c, j * 2 + core)

    def ctx_at(d):
        j = (c + d) % n_ctx
        return j, (j, t)

    loads = []
    for i, (src, dst) in enumerate(
        (
            (w_out_hbm, w_out),
            (shared_gate_hbm, shared_gate),
            (shared_up_hbm, shared_up),
            (shared_down_hbm, shared_down),
            (gate_up_hbm.at[0], gate_up),
            (down_hbm.at[0], down),
        )
    ):
        load = pltpu.make_async_copy(src, dst, load_sem.at[i])
        load.start()
        loads.append(load)

    barrier = pltpu.get_barrier_semaphore()

    def greet(device):
        pl.semaphore_signal(barrier, inc=1, device_id=device, device_id_type=MESH)

    loop(1, n_chip, lambda d: greet(chip_at(d)[1]))
    loop(1, n_ctx, lambda d: greet(ctx_at(d)[1]))
    greet(sibling)
    pl.semaphore_wait(barrier, n_chip + n_ctx - 1)

    lat[c, core, chip] = tail_ref[...]

    def ctx_copy(s, j, d):
        return remote(
            lat.at[s, core, chip],
            lat.at[s, core, chip],
            lat_ctx_send.at[d],
            lat_ctx_recv.at[s],
            (j, t),
        )

    loop(1, n_ctx - c, lambda d: ctx_copy(c, c + d, d).start())

    def tp_copy(s, d):
        _, device = chip_at(d)
        return remote(
            lat.at[s, core, chip],
            lat.at[s, core, chip],
            lat_tp_send.at[s, d],
            lat_tp_recv.at[s, chip],
            device,
        )

    def tp_wait(s, d):
        j, device = chip_at(d)
        remote(
            lat.at[s, core, j],
            lat.at[s, core, j],
            lat_tp_send.at[s, d],
            lat_tp_recv.at[s, j],
            device,
        ).wait_recv()

    loop(1, n_chip, lambda d: tp_copy(c, d).start())

    q_all = queries[...].reshape(n_chip, 2, rows, queries.shape[1])
    for k in range(2):
        q_half = q_all[:, k].reshape(half, queries.shape[1])
        for h in range(heads):
            piece = q_half[:, h * (NOPE + ROPE) : (h + 1) * (NOPE + ROPE)]
            q_s[h, k * half : (k + 1) * half, :] = jnp.concatenate(
                [piece, jnp.zeros((half, 2 * NOPE - NOPE - ROPE), BF16)], axis=1
            )
    top_s[...] = jnp.full(top_s.shape, LOW, F32)
    acc_s[...] = jnp.zeros(acc_s.shape, F32)

    def pass_on(i):
        s = c - i
        ctx_copy(s, (c + 1) % n_ctx, 0).wait_recv()
        loop(1, n_chip, lambda d: tp_copy(s, d).start())

    loop(1, c + 1, pass_on)

    scale = (1.0 / math.sqrt(NOPE + ROPE)) * math.log2(math.e)

    def place(index, axis_shape, axis):
        i = lax.broadcasted_iota(jnp.int32, axis_shape, axis) + index
        return ((i & (half - 1)) // rows) * (2 * rows) + (i // half) * rows + (i & (rows - 1))

    def attend(s, k, diagonal):
        block = lat[s, k].reshape(half, lat.shape[4])
        k_s[...] = dot(block[:, :latent], w_key[...]).astype(BF16)
        v_s[...] = dot(block[:, :latent], w_value[...]).astype(BF16)
        rope = block[:, latent:]
        ones = jnp.ones((half, VDIM), BF16)
        for h in range(heads):
            keys = jnp.concatenate([k_s[:, h * NOPE : (h + 1) * NOPE], rope], axis=1)
            values = jnp.concatenate([v_s[:, h * VDIM : (h + 1) * VDIM], ones], axis=1)
            scores = lax.dot_general(
                q_s[h], keys, (((1,), (1,)), ((), ())), preferred_element_type=F32
            )
            if diagonal:
                query_at = place(0, (group, half), 0)
                key_at = place(k * half, (group, half), 1)
                scores = jnp.where(key_at <= query_at, scores, LOW)
            top_old = top_s[h]
            top_new = jnp.maximum(top_old, jnp.max(scores, axis=1, keepdims=True))
            top_s[h] = top_new
            weights = jnp.concatenate(
                [
                    jnp.exp2((scores[:, j * 128 : (j + 1) * 128] - top_new) * scale).astype(BF16)
                    for j in range(half // 128)
                ],
                axis=1,
            )
            factor = jnp.exp2((top_old - top_new) * scale)
            factor = jnp.concatenate([factor, factor], axis=1)
            acc_s[h] = acc_s[h] * factor + dot(weights, values)

    def sib_copy(s, k):
        return remote(lat.at[s, k], lat.at[s, k], lat_sib_send.at[s], lat_sib_recv.at[s], sibling)

    def key_step(i, diagonal):
        s = c - i
        loop(1, n_chip, lambda d: tp_wait(s, d))
        sib_copy(s, core).start()

        def half_step(j):
            @pl.when(j == 1)
            def _():
                sib_copy(s, other).wait_recv()

            attend(s, (core + j) % 2, diagonal)

        loop(0, 2, half_step)

    key_step(0, True)
    loop(1, c + 1, lambda i: key_step(i, False))

    def sib_part(n, buffer, landing, send, recv, k):
        return remote(
            buffer.at[k, :, :, cols(n)],
            landing.at[:, :, cols(n)],
            send.at[n],
            recv.at[n],
            sibling,
        )

    def row_part(n, d, buffer, landing, send, recv):
        j, device = chip_at(d)
        return remote(
            buffer.at[core, j, :, cols(n)],
            landing.at[chip, :, cols(n)],
            send.at[n, d],
            recv.at[n, chip],
            device,
        )

    def row_wait(n, d, buffer, landing, send, recv):
        j, device = chip_at(d)
        remote(
            buffer.at[core, j, :, cols(n)],
            landing.at[j, :, cols(n)],
            send.at[n, d],
            recv.at[n, j],
            device,
        ).wait_recv()

    def pass_rows(n, buffer, from_sibling, landing, sib_send, sib_recv, send, recv):
        sib_part(n, buffer, from_sibling, sib_send, sib_recv, other).wait_recv()
        summed = (
            buffer[core, :, :, cols(n)].astype(F32) + from_sibling[:, :, cols(n)].astype(F32)
        ).astype(BF16)
        buffer[core, :, :, cols(n)] = summed
        landing[chip, :, cols(n)] = buffer[core, chip, :, cols(n)]
        loop(1, n_chip, lambda d: row_part(n, d, buffer, landing, send, recv).start())

    def sum_rows(n, buffer, landing, send, recv):
        loop(1, n_chip, lambda d: row_wait(n, d, buffer, landing, send, recv))
        return jnp.sum(landing[:, :, cols(n)].astype(F32), axis=0)

    attention = jnp.concatenate(
        [(acc_s[h, :, :VDIM] / acc_s[h, :, VDIM:]).astype(BF16) for h in range(heads)], axis=1
    )
    loads[0].wait()
    first = (part, sib_in, row_in, a_sib_send, a_sib_recv, a_row_send, a_row_recv)
    for n in range(CHUNKS):
        part[:, :, :, cols(n)] = (
            dot(attention, w_out[:, cols(n)]).astype(BF16).reshape(2, n_chip, rows, span)
        )
        sib_part(n, part, sib_in, a_sib_send, a_sib_recv, other).start()
        if n > 0:
            pass_rows(n - 1, *first)
    pass_rows(CHUNKS - 1, *first)

    meta = lat[c, :, :, :, latent:].reshape(group, lat.shape[4] - latent).astype(F32).T
    ids = meta[ROPE : ROPE + TOPK]
    gates_high = meta[ROPE + 8 : ROPE + 8 + TOPK]
    gates_low = meta[ROPE + 16 : ROPE + 16 + TOPK]
    expert_row = lax.broadcasted_iota(jnp.int32, (16, group), 0)
    expert = jnp.where(expert_row < n_ctx, expert_row * (2 * n_chip) + t, -1).astype(F32)
    member = jnp.zeros((16, group), F32)
    gate = jnp.zeros((16, group), F32)
    for k in range(TOPK):
        same = ids[k : k + 1] == expert
        member = member + jnp.where(same, 1.0, 0.0)
        gate = gate + jnp.where(same, gates_high[k : k + 1] + gates_low[k : k + 1], 0.0)
    before = lax.broadcasted_iota(jnp.int32, (group, group), 0) < lax.broadcasted_iota(
        jnp.int32, (group, group), 1
    )
    rank = dot(member.astype(BF16), jnp.where(before, 1.0, 0.0).astype(BF16))
    slot = lax.broadcasted_iota(jnp.int32, (slot_room, group), 0).astype(F32)
    for e in range(n_ctx):
        chosen = jnp.where(member[e : e + 1] > 0.5, rank[e : e + 1], -1.0) == slot
        pick[e] = jnp.where(chosen, 1.0, 0.0).astype(BF16)
        give[e] = jnp.where(chosen, gate[e : e + 1], 0.0).astype(BF16)

    for n in range(CHUNKS):
        hidden[:, cols(n)] = residual[:, cols(n)].astype(F32) + sum_rows(
            n, part, row_in, a_row_send, a_row_recv
        )
    state = hidden[...]
    mean_square = jnp.mean(state * state, axis=1, keepdims=True)
    normed[core, chip] = (state * lax.rsqrt(mean_square + 1e-06) * gain[...]).astype(BF16)

    def normed_copy(n, d, j):
        _, device = chip_at(d)
        return remote(
            normed.at[core, j, :, cols(n)],
            normed.at[core, j, :, cols(n)],
            n_send.at[n, d],
            n_recv.at[n, j],
            device,
        )

    def normed_sib(n, k):
        return remote(
            normed.at[k, :, :, cols(n)],
            normed.at[k, :, :, cols(n)],
            n_sib_send.at[n],
            n_sib_recv.at[n],
            sibling,
        )

    for n in range(CHUNKS):
        loop(1, n_chip, lambda d: normed_copy(n, d, chip).start())

    def slot_copy(n, d, source, landing, send, recv):
        j, device = ctx_at(d)
        return remote(
            source.at[j, :, cols(n)], landing.at[c, :, cols(n)], send.at[n, d], recv.at[n, c], device
        )

    def slot_wait(n, d, source, landing, send, recv):
        j, device = ctx_at(d)
        remote(
            source.at[j, :, cols(n)], landing.at[j, :, cols(n)], send.at[n, d], recv.at[n, j], device
        ).wait_recv()

    for n in range(CHUNKS):
        loop(1, n_chip, lambda d: normed_copy(n, d, chip_at(d)[0]).wait_recv())
        normed_sib(n, core).start()
        normed_sib(n, other).wait_recv()
        block = normed[:, :, :, cols(n)].reshape(group, span)
        picked = dot(pick[...].reshape(n_ctx * slot_room, group), block).astype(BF16)
        slots_out[:, :, cols(n)] = picked.reshape(n_ctx, slot_room, span)
        loop(1, n_ctx, lambda d: slot_copy(n, d, slots_out, slots_in, x_send, x_recv).start())
        slots_in[c, :, cols(n)] = slots_out[c, :, cols(n)]

    loads[1].wait()
    loads[2].wait()
    everyone = normed[...].reshape(group, width)
    gate_part = dot(everyone, shared_gate[...])
    up_part = dot(everyone, shared_up[...])
    shared_hidden = (gate_part / (1.0 + jnp.exp(-gate_part)) * up_part).astype(BF16)
    loads[3].wait()
    for n in range(CHUNKS):
        shared_acc[:, cols(n)] = dot(shared_hidden, shared_down[:, cols(n)])

    loads[4].wait()
    loads[5].wait()
    for n in range(CHUNKS):
        loop(1, n_ctx, lambda d: slot_wait(n, d, slots_out, slots_in, x_send, x_recv))
        items = slots_in[:, :, cols(n)].reshape(n_ctx * slot_room, span)
        product = dot(items, gate_up[cols(n), :])
        if n == 0:
            up_acc[...] = product
        else:
            up_acc[...] = up_acc[...] + product
    inner = down.shape[0]
    gate_part = up_acc[:, :inner]
    expert_hidden = (gate_part / (1.0 + jnp.exp(-gate_part)) * up_acc[:, inner:]).astype(BF16)
    for n in range(CHUNKS):
        result = dot(expert_hidden, down[:, cols(n)]).astype(BF16)
        back_out[:, :, cols(n)] = result.reshape(n_ctx, slot_room, span)
        loop(1, n_ctx, lambda d: slot_copy(n, d, back_out, back_in, y_send, y_recv).start())
        back_in[c, :, cols(n)] = back_out[c, :, cols(n)]

    give_rows = give[...].reshape(n_ctx * slot_room, group).astype(F32).T.astype(BF16)
    second = (part2, sib_in2, row_in2, b_sib_send, b_sib_recv, b_row_send, b_row_recv)
    for n in range(CHUNKS):
        loop(1, n_ctx, lambda d: slot_wait(n, d, back_out, back_in, y_send, y_recv))
        returned = back_in[:, :, cols(n)].reshape(n_ctx * slot_room, span)
        both = shared_acc[:, cols(n)] + dot(give_rows, returned)
        part2[:, :, :, cols(n)] = both.astype(BF16).reshape(2, n_chip, rows, span)
        sib_part(n, part2, sib_in2, b_sib_send, b_sib_recv, other).start()
        if n > 0:
            pass_rows(n - 1, *second)
    pass_rows(CHUNKS - 1, *second)
    for n in range(CHUNKS):
        out_ref[:, cols(n)] = (
            hidden[:, cols(n)] + sum_rows(n, part2, row_in2, b_row_send, b_row_recv)
        ).astype(BF16)

    loop(1, n_ctx - c, lambda d: ctx_copy(c, c + d, d).wait_send())

    def lat_sent(i):
        loop(1, n_chip, lambda d: tp_copy(c - i, d).wait_send())
        sib_copy(c - i, core).wait_send()

    loop(0, c + 1, lat_sent)
    for n in range(CHUNKS):
        sib_part(n, part, sib_in, a_sib_send, a_sib_recv, other).wait_send()
        sib_part(n, part2, sib_in2, b_sib_send, b_sib_recv, other).wait_send()
        normed_sib(n, core).wait_send()

        def sent(d):
            row_part(n, d, part, row_in, a_row_send, a_row_recv).wait_send()
            row_part(n, d, part2, row_in2, b_row_send, b_row_recv).wait_send()
            normed_copy(n, d, chip).wait_send()

        def slots_sent(d):
            slot_copy(n, d, slots_out, slots_in, x_send, x_recv).wait_send()
            slot_copy(n, d, back_out, back_in, y_send, y_recv).wait_send()

        loop(1, n_chip, sent)
        loop(1, n_ctx, slots_sent)


def shards(
    n_ctx,
    n_tp,
    queries,
    kv_latent,
    key_rope,
    w_key,
    w_value,
    w_out,
    residual,
    moe_gain,
    shared_gate,
    shared_up,
    shared_down,
    expert_gate_up,
    expert_down,
    expert_ids,
    gate_weights,
):
    rows, width = residual.shape
    n_chip = n_tp // 2
    heads = w_key.shape[1] // NOPE
    group = rows * n_tp
    latent = kv_latent.shape[1]
    slot_room = CAP * n_tp
    high = gate_weights.astype(BF16)
    low = (gate_weights - high.astype(F32)).astype(BF16)
    gap = jnp.zeros((rows, 8 - TOPK), BF16)
    row_tail = jnp.concatenate(
        [kv_latent, key_rope, expert_ids.astype(BF16), gap, high, gap, low, gap]
        + [jnp.zeros((rows, 128 - ROPE - 24), BF16)],
        axis=1,
    )
    dma = pltpu.SemaphoreType.DMA
    scratch = [
        pltpu.VMEM(w_out.shape, BF16),
        pltpu.VMEM(shared_gate.shape, BF16),
        pltpu.VMEM(shared_up.shape, BF16),
        pltpu.VMEM(shared_down.shape, BF16),
        pltpu.VMEM(expert_gate_up.shape[1:], BF16),
        pltpu.VMEM(expert_down.shape[1:], BF16),
        dma((6,)),
        pltpu.VMEM((n_ctx, 2, n_chip, rows, latent + 128), BF16),
        pltpu.VMEM((heads, group, 2 * NOPE), BF16),
        pltpu.VMEM((group // 2, heads * NOPE), BF16),
        pltpu.VMEM((group // 2, heads * VDIM), BF16),
        pltpu.VMEM((heads, group, 128), F32),
        pltpu.VMEM((heads, group, 2 * VDIM), F32),
        dma((n_ctx,)),
        dma((n_ctx,)),
        dma((n_ctx, n_chip)),
        dma((n_ctx, n_chip)),
        dma((n_ctx,)),
        dma((n_ctx,)),
        pltpu.VMEM((2, n_chip, rows, width), BF16),
        pltpu.VMEM((n_chip, rows, width), BF16),
        pltpu.VMEM((n_chip, rows, width), BF16),
        dma((CHUNKS,)),
        dma((CHUNKS,)),
        dma((CHUNKS, n_chip)),
        dma((CHUNKS, n_chip)),
        pltpu.VMEM((rows, width), F32),
        pltpu.VMEM((2, n_chip, rows, width), BF16),
        dma((CHUNKS, n_chip)),
        dma((CHUNKS, n_chip)),
        dma((CHUNKS,)),
        dma((CHUNKS,)),
        pltpu.VMEM((n_ctx, slot_room, group), BF16),
        pltpu.VMEM((n_ctx, slot_room, group), BF16),
        pltpu.VMEM((n_ctx, slot_room, width), BF16),
        pltpu.VMEM((n_ctx, slot_room, width), BF16),
        pltpu.VMEM((n_ctx * slot_room, expert_gate_up.shape[2]), F32),
        dma((CHUNKS, n_ctx)),
        dma((CHUNKS, n_ctx)),
        pltpu.VMEM((n_ctx, slot_room, width), BF16),
        pltpu.VMEM((n_ctx, slot_room, width), BF16),
        dma((CHUNKS, n_ctx)),
        dma((CHUNKS, n_ctx)),
        pltpu.VMEM((group, width), F32),
        pltpu.VMEM((2, n_chip, rows, width), BF16),
        pltpu.VMEM((n_chip, rows, width), BF16),
        pltpu.VMEM((n_chip, rows, width), BF16),
        dma((CHUNKS,)),
        dma((CHUNKS,)),
        dma((CHUNKS, n_chip)),
        dma((CHUNKS, n_chip)),
    ]
    vmem = pl.BlockSpec(memory_space=pltpu.VMEM)
    hbm = pl.BlockSpec(memory_space=pl.ANY)
    return pl.pallas_call(
        layer_kernel,
        out_shape=jax.ShapeDtypeStruct((rows, width), BF16),
        in_specs=[vmem, vmem, vmem, vmem, hbm, vmem, vmem, hbm, hbm, hbm, hbm, hbm],
        out_specs=vmem,
        scratch_shapes=scratch,
        compiler_params=pltpu.CompilerParams(
            collective_id=1, has_side_effects=True, vmem_limit_bytes=63 * 1024 * 1024
        ),
        cost_estimate=pl.CostEstimate(
            flops=20_000_000_000, bytes_accessed=20_000_000, transcendentals=9_000_000
        ),
        name="layer",
    )(
        row_tail,
        queries,
        w_key,
        w_value,
        w_out,
        residual,
        moe_gain.reshape(1, width),
        shared_gate,
        shared_up,
        shared_down,
        expert_gate_up,
        expert_down,
    )


def solution(mesh):
    in_specs = (
        P("ctx", "tp"),
        P(("ctx", "tp"), None),
        P(("ctx", "tp"), None),
        P(None, "tp"),
        P(None, "tp"),
        P("tp", None),
        P(("ctx", "tp"), None),
        P(),
        P(None, "tp"),
        P(None, "tp"),
        P("tp", None),
        P(("ctx", "tp"), None, None),
        P(("ctx", "tp"), None, None),
        P(("ctx", "tp"), None),
        P(("ctx", "tp"), None),
    )
    out_specs = P(("ctx", "tp"), None)
    return jax.shard_map(
        functools.partial(shards, mesh.shape["ctx"], mesh.shape["tp"]),
        mesh=mesh,
        in_specs=in_specs,
        out_specs=out_specs,
        check_vma=False,
    )
```

time: 514 us -> 163 us (0.32); the launches traced: 507 us -> 163 us
  waiting for transfers between devices: 156 us -> 0 us
  Pallas kernels: 0 us -> 152 us
  matrix products: 122 us -> 0 us
  blocking collectives: 86.5 us -> 0 us
  local copies, waits for them, and re-layouts: 71.7 us -> 9.15 us
  other arithmetic: 41.7 us -> 1.47 us
  starting transfers between devices: 16.6 us -> 0 us
  between operations: 13.3 us -> 0.03 us
    pallas_call x0 -> x1, Pallas kernels: none -> 152 us  [shards(): pl.pallas_call(layer_kernel, out_shape=jax.ShapeDtypeStruct((rows, width)...]
    dot_general x33 -> x0, matrix products: 122 us -> none  [the longest x8 35.8 us: attend_block(): jnp.einsum('shr,rhd->shd', weights.astype(jnp.bfloat16), value_heads, pre...]
    all_gather x3 -> x0, blocking collectives: 86.5 us -> none  [the longest x1 46.9 us: shards(): lax.all_gather(shard_rope, 'ctx', axis=0, tiled=True)]
    reduce_scatter x2 -> x0, waiting for transfers between devices: 62.8 us -> none  [the longest x1 62.8 us: shards(): lax.psum_scatter(jnp.dot(attention, w_out, preferred_element_type=jnp.flo...]
    all_gather x2 -> x0, waiting for transfers between devices: 54.2 us -> none  [the longest x1 38.1 us: shards(): normed_block = lax.all_gather(normed, 'tp', axis=0, tiled=True)]
    all_to_all x2 -> x0, waiting for transfers between devices: 38.7 us -> none  [the longest x1 38.7 us: shards(): lax.all_to_all(expert_output.reshape(item_shape), ('ctx', 'tp'), split_ax...]
    dynamic_slice x24 -> x0, local copies, waits for them, and re-layouts: 34.7 us -> none  [the longest x16 26.5 us: advance(): lax.dynamic_slice_in_dim(values, offset, block_rows, 0)]
    reduce_sum x11 -> x0, other arithmetic: 25 us -> none  [the longest x8 23.7 us: attend_block(): total_new = total_old * factor + jnp.sum(weights, axis=2)]
  transfers between devices with their start and end apart: 6 -> 0, of which waited for: 4 -> 0; matrix products, arithmetic and copies ran while one was open for 10% -> 0% of each run, Pallas kernels for 0% -> 0%
where the time goes in v1:
time: 163 us
  Pallas kernels  152 us (93%)
  local copies, waits for them, and re-layouts  9.15 us (6%)
    pallas_call x1, Pallas kernels, shards(): pl.pallas_call(layer_kernel, out_shape=jax.ShapeDtypeStruct((rows, width)...  152 us
    unnamed x6, local copies, waits for them, and re-layouts  6.16 us

profile of v1, /device:TPU:16, one launch (start us, length us, event | category | flops | bytes accessed | tf_op | source)
XLA Modules:
  0.0 162.7 jit_solution(5208676244175572123)
XLA Ops:
  0.0 0.0 copy-start
  0.0 0.8 convert_element_type.12
  0.8 0.7 convert_element_type.13
  1.5 0.1 copy.24
  1.6 0.1 copy.23
  1.7 1.3 reshape.3.gain
  3.0 0.8 copy.22
  3.8 1.5 concatenate.3.tail_ref
  5.2 2.4 %copy.25.shared_gate_hbm = bf16[2560,192]{1,0:T(8,128)(2,1)} copy(bf16[2560,192]{0,1:T(8,128)(2,1)} %param.23) | data formatting | bytes 1966080 | tf_op args[8]
  7.6 0.0 copy-done
  7.6 1.4 copy.26.shared_up_hbm
  9.0 152.0 %layer.1 = bf16[32,2560]{1,0:T(8,128)(2,1)} custom-call(bf16[32,640]{1,0:T(8,128)(2,1)} %concatenate.3.tail_ref, bf16[512,768]{1,0:T(8,128)(2,1)} %queries.1, bf16[512,512]{1,0:T(8,128)(2,1)} %w_key.1, bf16[512,512]{1,0:T(8,128)(2,1)} %w_value.1, bf16[512,2560]{1,0:T(8,128)(2,1)} %w_out_hbm.1, bf16[32,2560]{1,0:T(8,128)(2,1)} %residual.1, ...), custom_call_target="tpu_custom_call" | custom-call | flops 20000000000 | bytes 20000000 | tf_op jit(solution)/shard_map/layer/pallas_call | solution.py:561
  161.1 1.6 copy.28
  (3 shorter events, 0.0 us)
Async XLA Ops:
  0.0 7.6 %copy-start = (bf16[2560,192]{0,1:T(8,128)(2,1)S(1)}, bf16[2560,192]{0,1:T(8,128)(2,1)}, u32[]{:S(2)}) copy-start(bf16[2560,192]{0,1:T(8,128)(2,1)} %param.24) | copy-start | bytes 2949124

commit v2 on v1

v2 whole, which is shorter than its diff:
```python
import functools
import math

import jax
import jax.numpy as jnp
from jax import lax
from jax.experimental import pallas as pl
from jax.experimental.pallas import tpu as pltpu
from jax.sharding import PartitionSpec as P

NOPE = 128
ROPE = 64
VDIM = 128
TOPK = 6
CAP = 3
MESH = pl.DeviceIdType.MESH
F32 = jnp.float32
BF16 = jnp.bfloat16
LOW = -1e30
CHUNKS = 5


def loop(first, end, body):
    if isinstance(first, int) and isinstance(end, int):
        for i in range(first, end):
            body(i)
        return

    def step(i, carry):
        body(i)
        return carry

    lax.fori_loop(first, end, step, 0)


def dot(a, b):
    return jnp.dot(a, b, preferred_element_type=F32)


def dot_rows(a, b):
    return lax.dot_general(a, b, (((1,), (1,)), ((), ())), preferred_element_type=F32)


def layer_kernel(
    queries_hbm,
    kv_latent_hbm,
    key_rope_hbm,
    w_key_hbm,
    w_value_hbm,
    w_out_hbm,
    residual_hbm,
    gain_hbm,
    shared_gate_hbm,
    shared_up_hbm,
    shared_down_hbm,
    gate_up_hbm,
    down_hbm,
    ids_hbm,
    gates_hbm,
    out_ref,
    kv_latent,
    key_rope,
    ids_ref,
    gates_ref,
    queries,
    w_key,
    w_value,
    residual,
    gain,
    w_out,
    shared_gate,
    shared_up,
    shared_down,
    gate_up,
    down,
    load_sem,
    lat,
    q_s,
    k_s,
    v_s,
    top_s,
    acc_s,
    lat_ctx_send,
    lat_ctx_recv,
    lat_tp_send,
    lat_tp_recv,
    lat_sib_send,
    lat_sib_recv,
    part,
    sib_in,
    row_in,
    a_sib_send,
    a_sib_recv,
    a_row_send,
    a_row_recv,
    hidden,
    normed,
    n_send,
    n_recv,
    n_sib_send,
    n_sib_recv,
    pick,
    give,
    slots_out,
    slots_in,
    up_acc,
    x_send,
    x_recv,
    back_out,
    back_in,
    y_send,
    y_recv,
    shared_acc,
    part2,
    sib_in2,
    row_in2,
    b_sib_send,
    b_sib_recv,
    b_row_send,
    b_row_recv,
):
    c = lax.axis_index("ctx")
    t = lax.axis_index("tp")
    chip = t // 2
    core = t % 2
    other = 1 - core
    sibling = (c, chip * 2 + other)
    rows = residual.shape[0]
    width = residual.shape[1]
    heads = q_s.shape[0]
    latent = w_key.shape[0]
    n_ctx, _, n_chip = lat.shape[:3]
    half = n_chip * rows
    group = 2 * half
    span = width // CHUNKS
    slot_room = slots_out.shape[1]

    def cols(n):
        return pl.ds(n * span, span)

    def remote(src, dst, send, recv, device):
        return pltpu.make_async_remote_copy(
            src_ref=src,
            dst_ref=dst,
            send_sem=send,
            recv_sem=recv,
            device_id=device,
            device_id_type=MESH,
        )

    def chip_at(d):
        j = (chip + d) % n_chip
        return j, (c, j * 2 + core)

    def across(j):
        return ((j + c) % 2) * (n_chip // 2)

    def ctx_at(d):
        j = (c + d) % n_ctx
        return j, (j, ((chip + across(j)) % n_chip) * 2 + core)

    loads = []
    for i, (src, dst) in enumerate(
        (
            (kv_latent_hbm, kv_latent),
            (key_rope_hbm, key_rope),
            (ids_hbm, ids_ref),
            (gates_hbm, gates_ref),
            (queries_hbm, queries),
            (w_key_hbm, w_key),
            (w_value_hbm, w_value),
            (residual_hbm, residual),
            (gain_hbm, gain),
            (w_out_hbm, w_out),
            (shared_gate_hbm, shared_gate),
            (shared_up_hbm, shared_up),
            (shared_down_hbm, shared_down),
            (gate_up_hbm.at[0], gate_up),
            (down_hbm.at[0], down),
        )
    ):
        load = pltpu.make_async_copy(src, dst, load_sem.at[i])
        loads.append(load)
    for load in loads[:9]:
        load.start()
    loaded = set()

    def use(i):
        loaded.add(i)
        loads[i].wait()

    pending = []

    def finish():
        for i in range(len(loads)):
            if i not in loaded and (i < 9 or len(pending) > 1 or (pending and i < 10)):
                use(i)
        for wait in pending:
            wait()

    barrier = pltpu.get_barrier_semaphore()

    def greet(device):
        pl.semaphore_signal(barrier, inc=1, device_id=device, device_id_type=MESH)

    loop(1, n_chip, lambda d: greet(chip_at(d)[1]))
    loop(1, n_ctx, lambda d: greet(ctx_at(d)[1]))
    greet(sibling)
    pl.semaphore_wait(barrier, n_chip + n_ctx - 1)

    for i in range(4):
        use(i)
    lat[c, core, chip, :, :latent] = kv_latent[...]
    gates = gates_ref[...]
    gates_high = gates.astype(BF16).astype(F32)
    tail = jnp.concatenate(
        [
            jnp.zeros((ROPE, rows), F32),
            ids_ref[...].astype(F32),
            gates_high,
            gates - gates_high,
            jnp.zeros((ROPE - 3 * TOPK, rows), F32),
        ],
        axis=0,
    ).T
    lat[c, core, chip, :, latent:] = jnp.concatenate(
        [key_rope[...], tail[:, ROPE:].astype(BF16)], axis=1
    )

    def block_copy(s, d):
        held = (chip + across(s)) % n_chip
        return remote(
            lat.at[s, core, held],
            lat.at[s, core, held],
            lat_ctx_send.at[d],
            lat_ctx_recv.at[s],
            ctx_at(d)[1],
        )

    def half_copy(s, d):
        return remote(
            lat.at[s, core],
            lat.at[s, core],
            lat_ctx_send.at[d],
            lat_ctx_recv.at[s],
            ctx_at(d)[1],
        )

    odd_later = (n_ctx - c) // 2
    even_later = (n_ctx - 1 - c) // 2
    loop(0, odd_later, lambda i: block_copy(c, 2 * i + 1).start())

    def tp_copy(s, d):
        held = (chip + across(s)) % n_chip
        return remote(
            lat.at[s, core, held],
            lat.at[s, core, held],
            lat_tp_send.at[s],
            lat_tp_recv.at[s],
            chip_at(d)[1],
        )

    def tp_all(s):
        blocks = lat.at[s, core, pl.ds(0, n_chip - 1)]
        return remote(blocks, blocks, lat_tp_send.at[s], lat_tp_recv.at[s], sibling)

    loop(1, n_chip, lambda d: tp_copy(c, d).start())

    use(4)
    q_all = queries[...].reshape(n_chip, 2, rows, queries.shape[1])
    for k in range(2):
        q_half = q_all[:, k].reshape(half, queries.shape[1])
        for h in range(heads):
            piece = q_half[:, h * (NOPE + ROPE) : (h + 1) * (NOPE + ROPE)]
            q_s[h, k * half : (k + 1) * half, :] = jnp.concatenate(
                [piece, jnp.zeros((half, 2 * NOPE - NOPE - ROPE), BF16)], axis=1
            )
    top_s[...] = jnp.full(top_s.shape, LOW, F32)
    acc_s[...] = jnp.zeros(acc_s.shape, F32)

    def pass_on(i):
        s = c - 2 * i - 1
        block_copy(s, 1).wait_recv()
        loop(1, n_chip, lambda d: tp_copy(s, d).start())

    loop(0, (c + 1) // 2, pass_on)

    def lat_sent():
        loop(0, odd_later, lambda i: block_copy(c, 2 * i + 1).wait_send())
        loop(0, even_later, lambda i: half_copy(c, 2 * i + 2).wait_send())
        tp_all(c).wait_send()
        loop(0, (c + 1) // 2, lambda i: tp_all(c - 2 * i - 1).wait_send())
        loop(0, c + 1, lambda i: sib_copy(c - i, core).wait_send())

    pending.append(lat_sent)

    scale = (1.0 / math.sqrt(NOPE + ROPE)) * math.log2(math.e)

    def place(index, axis_shape, axis):
        i = lax.broadcasted_iota(jnp.int32, axis_shape, axis) + index
        return ((i & (half - 1)) // rows) * (2 * rows) + (i // half) * rows + (i & (rows - 1))

    def attend(s, k, diagonal):
        block = lat[s, k].reshape(half, lat.shape[4])
        k_s[...] = dot(block[:, :latent], w_key[...]).astype(BF16)
        v_s[...] = dot(block[:, :latent], w_value[...]).astype(BF16)
        rope = block[:, latent:]
        ones = jnp.ones((half, VDIM), BF16)
        for h in range(heads):
            keys = jnp.concatenate([k_s[:, h * NOPE : (h + 1) * NOPE], rope], axis=1)
            values = jnp.concatenate([v_s[:, h * VDIM : (h + 1) * VDIM], ones], axis=1)
            scores = dot_rows(q_s[h], keys)
            if diagonal:
                query_at = place(0, (group, half), 0)
                key_at = place(k * half, (group, half), 1)
                scores = jnp.where(key_at <= query_at, scores, LOW)
            top_old = top_s[h]
            top_new = jnp.maximum(top_old, jnp.max(scores, axis=1, keepdims=True))
            top_s[h] = top_new
            weights = jnp.concatenate(
                [
                    jnp.exp2((scores[:, j * 128 : (j + 1) * 128] - top_new) * scale).astype(BF16)
                    for j in range(half // 128)
                ],
                axis=1,
            )
            factor = jnp.exp2((top_old - top_new) * scale)
            factor = jnp.concatenate([factor, factor], axis=1)
            acc_s[h] = acc_s[h] * factor + dot(weights, values)

    def sib_copy(s, k):
        return remote(lat.at[s, k], lat.at[s, k], lat_sib_send.at[s], lat_sib_recv.at[s], sibling)

    def key_step(i, diagonal):
        s = c - i
        if diagonal:
            tp_all(s).wait_recv()
            loop(0, even_later, lambda i: half_copy(c, 2 * i + 2).start())
        else:

            @pl.when(i % 2 == 1)
            def _():
                tp_all(s).wait_recv()

            @pl.when(i % 2 == 0)
            def _():
                half_copy(s, 2).wait_recv()

        sib_copy(s, core).start()

        def half_step(j):
            @pl.when(j == 1)
            def _():
                sib_copy(s, other).wait_recv()

            attend(s, (core + j) % 2, diagonal)

        loop(0, 2, half_step)

    use(5)
    use(6)
    key_step(0, True)
    loads[9].start()
    loop(1, c + 1, lambda i: key_step(i, False))

    def sib_part(n, buffer, landing, send, recv):
        return remote(
            buffer.at[other, :, :, cols(n)],
            landing.at[:, :, cols(n)],
            send.at[0],
            recv.at[n],
            sibling,
        )

    def row_part(n, d, buffer, landing, send, recv):
        j, device = chip_at(d)
        return remote(
            buffer.at[core, j, :, cols(n)],
            landing.at[chip, :, cols(n)],
            send.at[0],
            recv.at[n],
            device,
        )

    def pass_rows(n, buffer, from_sibling, landing, sib_send, sib_recv, send, recv):
        sib_part(n, buffer, from_sibling, sib_send, sib_recv).wait_recv()
        summed = (
            buffer[core, :, :, cols(n)].astype(F32) + from_sibling[:, :, cols(n)].astype(F32)
        ).astype(BF16)
        buffer[core, :, :, cols(n)] = summed
        landing[chip, :, cols(n)] = buffer[core, chip, :, cols(n)]
        loop(1, n_chip, lambda d: row_part(n, d, buffer, landing, send, recv).start())

    def rows_sent(buffer, from_sibling, landing, sib_send, sib_recv, send, recv):
        remote(
            buffer.at[other], from_sibling, sib_send.at[0], sib_recv.at[0], sibling
        ).wait_send()
        others = pl.ds(0, n_chip - 1)
        remote(
            buffer.at[core, others], landing.at[others], send.at[0], recv.at[0], sibling
        ).wait_send()

    def sum_rows(n, landing, send, recv):
        blocks = landing.at[pl.ds(0, n_chip - 1), :, cols(n)]
        remote(blocks, blocks, send.at[0], recv.at[n], sibling).wait_recv()
        return jnp.sum(landing[:, :, cols(n)].astype(F32), axis=0)

    attention = jnp.concatenate(
        [(acc_s[h, :, :VDIM] / acc_s[h, :, VDIM:]).astype(BF16) for h in range(heads)], axis=1
    )
    use(9)
    first = (part, sib_in, row_in, a_sib_send, a_sib_recv, a_row_send, a_row_recv)
    for n in range(CHUNKS):
        part[:, :, :, cols(n)] = (
            dot(attention, w_out[:, cols(n)]).astype(BF16).reshape(2, n_chip, rows, span)
        )
        sib_part(n, part, sib_in, a_sib_send, a_sib_recv).start()
        if n > 0:
            pass_rows(n - 1, *first)
    pass_rows(CHUNKS - 1, *first)
    pending.append(functools.partial(rows_sent, *first))

    for load in loads[10:]:
        load.start()

    meta = lat[c, :, :, :, latent:].reshape(group, lat.shape[4] - latent).astype(F32).T
    ids = meta[ROPE : ROPE + TOPK]
    gates_all = meta[ROPE + TOPK : ROPE + 2 * TOPK] + meta[ROPE + 2 * TOPK : ROPE + 3 * TOPK]
    expert_row = lax.broadcasted_iota(jnp.int32, (16, group), 0)
    owner = expert_row * (2 * n_chip) + ((chip + across(expert_row)) % n_chip) * 2 + core
    expert = jnp.where(expert_row < n_ctx, owner, -1).astype(F32)
    member = jnp.zeros((16, group), F32)
    gate = jnp.zeros((16, group), F32)
    for k in range(TOPK):
        same = ids[k : k + 1] == expert
        member = member + jnp.where(same, 1.0, 0.0)
        gate = gate + jnp.where(same, gates_all[k : k + 1], 0.0)
    before = lax.broadcasted_iota(jnp.int32, (group, group), 0) < lax.broadcasted_iota(
        jnp.int32, (group, group), 1
    )
    rank = dot(member.astype(BF16), jnp.where(before, 1.0, 0.0).astype(BF16))
    slot = lax.broadcasted_iota(jnp.int32, (slot_room, group), 0).astype(F32)
    for e in range(n_ctx):
        chosen = jnp.where(member[e : e + 1] > 0.5, rank[e : e + 1], -1.0) == slot
        pick[e] = jnp.where(chosen, 1.0, 0.0).astype(BF16)
        give[e] = jnp.where(chosen, gate[e : e + 1], 0.0).astype(BF16)

    use(7)
    use(8)
    for n in range(CHUNKS):
        hidden[:, cols(n)] = residual[:, cols(n)].astype(F32) + sum_rows(
            n, row_in, a_row_send, a_row_recv
        )
    state = hidden[...]
    mean_square = jnp.mean(state * state, axis=1, keepdims=True)
    normed[core, chip] = (state * lax.rsqrt(mean_square + 1e-06) * gain[...].reshape(1, width)).astype(BF16)

    def normed_copy(n, d):
        block = normed.at[core, chip, :, cols(n)]
        return remote(block, block, n_send.at[0], n_recv.at[n], chip_at(d)[1])

    def normed_all(n):
        blocks = normed.at[core, pl.ds(0, n_chip - 1), :, cols(n)]
        return remote(blocks, blocks, n_send.at[0], n_recv.at[n], sibling)

    def normed_sib(n):
        half_rows = normed.at[core, :, :, cols(n)]
        return remote(half_rows, half_rows, n_sib_send.at[0], n_sib_recv.at[n], sibling)

    def normed_sent():
        blocks = normed.at[core, pl.ds(0, n_chip - 1)]
        remote(blocks, blocks, n_send.at[0], n_recv.at[0], sibling).wait_send()
        half_rows = normed.at[core]
        remote(half_rows, half_rows, n_sib_send.at[0], n_sib_recv.at[0], sibling).wait_send()

    for n in range(CHUNKS):
        loop(1, n_chip, lambda d: normed_copy(n, d).start())
    pending.append(normed_sent)

    def slot_copy(n, d, source, landing, send, recv):
        j, device = ctx_at(d)
        return remote(
            source.at[j, :, cols(n)], landing.at[c, :, cols(n)], send.at[0], recv.at[n], device
        )

    def slot_wait(n, source, landing, send, recv):
        blocks = landing.at[pl.ds(0, n_ctx - 1), :, cols(n)]
        remote(blocks, blocks, send.at[0], recv.at[n], sibling).wait_recv()

    def slots_sent(source, landing, send, recv):
        blocks = source.at[pl.ds(0, n_ctx - 1)]
        remote(blocks, blocks, send.at[0], recv.at[0], sibling).wait_send()

    there = (slots_out, slots_in, x_send, x_recv)
    back = (back_out, back_in, y_send, y_recv)
    for n in range(CHUNKS):
        normed_all(n).wait_recv()
        normed_sib(n).start()
        normed_sib(n).wait_recv()
        block = normed[:, :, :, cols(n)].reshape(group, span)
        picked = dot(pick[...].reshape(n_ctx * slot_room, group), block).astype(BF16)
        slots_out[:, :, cols(n)] = picked.reshape(n_ctx, slot_room, span)
        loop(1, n_ctx, lambda d: slot_copy(n, d, *there).start())
        slots_in[c, :, cols(n)] = slots_out[c, :, cols(n)]
    pending.append(functools.partial(slots_sent, *there))

    use(10)
    use(11)
    everyone = normed[...].reshape(group, width)
    gate_part = dot_rows(everyone, shared_gate[...])
    up_part = dot_rows(everyone, shared_up[...])
    shared_hidden = (gate_part / (1.0 + jnp.exp(-gate_part)) * up_part).astype(BF16)
    use(12)
    for n in range(CHUNKS):
        shared_acc[:, cols(n)] = dot(shared_hidden, shared_down[:, cols(n)])

    use(13)
    use(14)
    for n in range(CHUNKS):
        slot_wait(n, *there)
        items = slots_in[:, :, cols(n)].reshape(n_ctx * slot_room, span)
        product = dot(items, gate_up[cols(n), :])
        if n == 0:
            up_acc[...] = product
        else:
            up_acc[...] = up_acc[...] + product
    inner = down.shape[0]
    gate_part = up_acc[:, :inner]
    expert_hidden = (gate_part / (1.0 + jnp.exp(-gate_part)) * up_acc[:, inner:]).astype(BF16)
    for n in range(CHUNKS):
        result = dot(expert_hidden, down[:, cols(n)]).astype(BF16)
        back_out[:, :, cols(n)] = result.reshape(n_ctx, slot_room, span)
        loop(1, n_ctx, lambda d: slot_copy(n, d, *back).start())
        back_in[c, :, cols(n)] = back_out[c, :, cols(n)]
    pending.append(functools.partial(slots_sent, *back))

    give_rows = give[...].reshape(n_ctx * slot_room, group).astype(F32).T.astype(BF16)
    second = (part2, sib_in2, row_in2, b_sib_send, b_sib_recv, b_row_send, b_row_recv)
    for n in range(CHUNKS):
        slot_wait(n, *back)
        returned = back_in[:, :, cols(n)].reshape(n_ctx * slot_room, span)
        both = shared_acc[:, cols(n)] + dot(give_rows, returned)
        part2[:, :, :, cols(n)] = both.astype(BF16).reshape(2, n_chip, rows, span)
        sib_part(n, part2, sib_in2, b_sib_send, b_sib_recv).start()
        if n > 0:
            pass_rows(n - 1, *second)
    pass_rows(CHUNKS - 1, *second)
    pending.append(functools.partial(rows_sent, *second))
    for n in range(CHUNKS):
        out_ref[:, cols(n)] = (
            hidden[:, cols(n)] + sum_rows(n, row_in2, b_row_send, b_row_recv)
        ).astype(BF16)

    finish()


def shards(
    n_ctx,
    n_tp,
    queries,
    kv_latent,
    key_rope,
    w_key,
    w_value,
    w_out,
    residual,
    moe_gain,
    shared_gate,
    shared_up,
    shared_down,
    expert_gate_up,
    expert_down,
    expert_ids,
    gate_weights,
):
    rows, width = residual.shape
    n_chip = n_tp // 2
    heads = w_key.shape[1] // NOPE
    group = rows * n_tp
    latent = kv_latent.shape[1]
    slot_room = CAP * n_tp
    dma = pltpu.SemaphoreType.DMA
    scratch = [
        pltpu.VMEM(kv_latent.shape, BF16),
        pltpu.VMEM(key_rope.shape, BF16),
        pltpu.VMEM(expert_ids.shape[::-1], jnp.int32),
        pltpu.VMEM(gate_weights.shape[::-1], F32),
        pltpu.VMEM(queries.shape, BF16),
        pltpu.VMEM(w_key.shape, BF16),
        pltpu.VMEM(w_value.shape, BF16),
        pltpu.VMEM(residual.shape, BF16),
        pltpu.VMEM(moe_gain.shape, F32),
        pltpu.VMEM(w_out.shape, BF16),
        pltpu.VMEM(shared_gate.shape[::-1], BF16),
        pltpu.VMEM(shared_up.shape[::-1], BF16),
        pltpu.VMEM(shared_down.shape, BF16),
        pltpu.VMEM(expert_gate_up.shape[1:], BF16),
        pltpu.VMEM(expert_down.shape[1:], BF16),
        dma((15,)),
        pltpu.VMEM((n_ctx, 2, n_chip, rows, latent + 128), BF16),
        pltpu.VMEM((heads, group, 2 * NOPE), BF16),
        pltpu.VMEM((group // 2, heads * NOPE), BF16),
        pltpu.VMEM((group // 2, heads * VDIM), BF16),
        pltpu.VMEM((heads, group, 128), F32),
        pltpu.VMEM((heads, group, 2 * VDIM), F32),
        dma((n_ctx,)),
        dma((n_ctx,)),
        dma((n_ctx,)),
        dma((n_ctx,)),
        dma((n_ctx,)),
        dma((n_ctx,)),
        pltpu.VMEM((2, n_chip, rows, width), BF16),
        pltpu.VMEM((n_chip, rows, width), BF16),
        pltpu.VMEM((n_chip, rows, width), BF16),
        dma((1,)),
        dma((CHUNKS,)),
        dma((1,)),
        dma((CHUNKS,)),
        pltpu.VMEM((rows, width), F32),
        pltpu.VMEM((2, n_chip, rows, width), BF16),
        dma((1,)),
        dma((CHUNKS,)),
        dma((1,)),
        dma((CHUNKS,)),
        pltpu.VMEM((n_ctx, slot_room, group), BF16),
        pltpu.VMEM((n_ctx, slot_room, group), BF16),
        pltpu.VMEM((n_ctx, slot_room, width), BF16),
        pltpu.VMEM((n_ctx, slot_room, width), BF16),
        pltpu.VMEM((n_ctx * slot_room, expert_gate_up.shape[2]), F32),
        dma((1,)),
        dma((CHUNKS,)),
        pltpu.VMEM((n_ctx, slot_room, width), BF16),
        pltpu.VMEM((n_ctx, slot_room, width), BF16),
        dma((1,)),
        dma((CHUNKS,)),
        pltpu.VMEM((group, width), F32),
        pltpu.VMEM((2, n_chip, rows, width), BF16),
        pltpu.VMEM((n_chip, rows, width), BF16),
        pltpu.VMEM((n_chip, rows, width), BF16),
        dma((1,)),
        dma((CHUNKS,)),
        dma((1,)),
        dma((CHUNKS,)),
    ]
    vmem = pl.BlockSpec(memory_space=pltpu.VMEM)
    hbm = pl.BlockSpec(memory_space=pl.ANY)
    return pl.pallas_call(
        layer_kernel,
        out_shape=jax.ShapeDtypeStruct((rows, width), BF16),
        in_specs=[hbm] * 15,
        out_specs=vmem,
        scratch_shapes=scratch,
        compiler_params=pltpu.CompilerParams(
            collective_id=1, has_side_effects=True, vmem_limit_bytes=63 * 1024 * 1024
        ),
        cost_estimate=pl.CostEstimate(
            flops=20_000_000_000, bytes_accessed=20_000_000, transcendentals=9_000_000
        ),
        name="layer",
    )(
        queries,
        kv_latent,
        key_rope,
        w_key,
        w_value,
        w_out,
        residual,
        moe_gain,
        shared_gate.T,
        shared_up.T,
        shared_down,
        expert_gate_up,
        expert_down,
        expert_ids.T,
        gate_weights.T,
    )


def solution(mesh):
    in_specs = (
        P("ctx", "tp"),
        P(("ctx", "tp"), None),
        P(("ctx", "tp"), None),
        P(None, "tp"),
        P(None, "tp"),
        P("tp", None),
        P(("ctx", "tp"), None),
        P(),
        P(None, "tp"),
        P(None, "tp"),
        P("tp", None),
        P(("ctx", "tp"), None, None),
        P(("ctx", "tp"), None, None),
        P(("ctx", "tp"), None),
        P(("ctx", "tp"), None),
    )
    out_specs = P(("ctx", "tp"), None)
    return jax.shard_map(
        functools.partial(shards, mesh.shape["ctx"], mesh.shape["tp"]),
        mesh=mesh,
        in_specs=in_specs,
        out_specs=out_specs,
        check_vma=False,
    )
```

time: 163 us -> 125 us (0.77); the launches traced: 163 us -> 122 us
  Pallas kernels: 152 us -> 121 us
  local copies, waits for them, and re-layouts: 9.15 us -> 1.59 us
    pallas_call x1, Pallas kernels: 152 us -> 121 us  [shards(): pl.pallas_call(layer_kernel, out_shape=jax.ShapeDtypeStruct((rows, width)...]
    unnamed x6 -> x1, local copies, waits for them, and re-layouts: 6.16 us -> 1.59 us
where the time goes in v2:
time: 125 us; the launch traced here: 122 us
  Pallas kernels  121 us (97%)
  local copies, waits for them, and re-layouts  1.59 us (1%)
    pallas_call x1, Pallas kernels, shards(): pl.pallas_call(layer_kernel, out_shape=jax.ShapeDtypeStruct((rows, width)...  121 us

profile of v2, /device:TPU:16, one launch (start us, length us, event | category | flops | bytes accessed | tf_op | source)
XLA Modules:
  0.0 122.2 jit_solution(8724999665150526894)
XLA Ops:
  0.0 120.6 %layer.1 = bf16[32,2560]{1,0:T(8,128)(2,1)} custom-call(bf16[512,768]{1,0:T(8,128)(2,1)} %queries_hbm.1, bf16[32,512]{1,0:T(8,128)(2,1)} %kv_latent_hbm.1, bf16[32,64]{1,0:T(8,128)(2,1)} %key_rope_hbm.1, bf16[512,512]{1,0:T(8,128)(2,1)} %w_key_hbm.1, bf16[512,512]{1,0:T(8,128)(2,1)} %w_value_hbm.1, bf16[512,2560]{1,0:T(8,128)(2,1)} %w_out_hbm.1, ...), custom_call_target="tpu_custom_call" | custom-call | flops 20000000000 | bytes 20000000 | tf_op jit(solution)/shard_map/layer/pallas_call | solution.py:647
  120.6 1.6 %copy.17 = bf16[32,2560]{1,0:T(8,128)(2,1)} copy(bf16[32,2560]{1,0:T(8,128)(2,1)} %layer.1) | data formatting | bytes 327680

commit v3 on v2

--- a/solution.py
+++ b/solution.py
@@ -17,7 +17,8 @@
 F32 = jnp.float32
 BF16 = jnp.bfloat16
 LOW = -1e30
-CHUNKS = 5
+CHUNKS = 10
+LEAD = 3
 
 
 def loop(first, end, body):
@@ -246,9 +247,10 @@
             ctx_at(d)[1],
         )
 
-    odd_later = (n_ctx - c) // 2
-    even_later = (n_ctx - 1 - c) // 2
-    loop(0, odd_later, lambda i: block_copy(c, 2 * i + 1).start())
+    odd = c % 2
+    later = (n_ctx - 1 - c) // 2
+    earlier = c // 2
+    loop(0, later, lambda i: block_copy(c, 2 * (later - i) + 1 - 2 * odd).start())
 
     def tp_copy(s, d):
         held = (chip + across(s)) % n_chip
@@ -279,17 +281,22 @@
     acc_s[...] = jnp.zeros(acc_s.shape, F32)
 
     def pass_on(i):
-        s = c - 2 * i - 1
+        s = c - 2 * i - 1 - 2 * odd
         block_copy(s, 1).wait_recv()
         loop(1, n_chip, lambda d: tp_copy(s, d).start())
 
-    loop(0, (c + 1) // 2, pass_on)
+    loop(0, earlier, pass_on)
 
     def lat_sent():
-        loop(0, odd_later, lambda i: block_copy(c, 2 * i + 1).wait_send())
-        loop(0, even_later, lambda i: half_copy(c, 2 * i + 2).wait_send())
+        loop(0, later, lambda i: block_copy(c, 2 * (later - i) + 1 - 2 * odd).wait_send())
+        loop(0, later, lambda i: half_copy(c, 2 * (later - i)).wait_send())
+
+        @pl.when(odd == 0)
+        def _():
+            half_copy(c, 1).wait_send()
+
         tp_all(c).wait_send()
-        loop(0, (c + 1) // 2, lambda i: tp_all(c - 2 * i - 1).wait_send())
+        loop(0, earlier, lambda i: tp_all(c - 2 * i - 1 - 2 * odd).wait_send())
         loop(0, c + 1, lambda i: sib_copy(c - i, core).wait_send())
 
     pending.append(lat_sent)
@@ -331,18 +338,28 @@
     def sib_copy(s, k):
         return remote(lat.at[s, k], lat.at[s, k], lat_sib_send.at[s], lat_sib_recv.at[s], sibling)
 
-    def key_step(i, diagonal):
-        s = c - i
+    def key_step(q, diagonal):
         if diagonal:
+            s = c
             tp_all(s).wait_recv()
-            loop(0, even_later, lambda i: half_copy(c, 2 * i + 2).start())
+
+            @pl.when(odd == 0)
+            def _():
+                half_copy(c, 1).start()
+
+            loop(0, later, lambda i: half_copy(c, 2 * (later - i)).start())
         else:
-
-            @pl.when(i % 2 == 1)
+            whole = q // (earlier + 1)
+            r = jnp.maximum(q - earlier, 1)
+            across_whole = odd * (1 // r)
+            back = (1 - whole) * (2 * q - 1 + 2 * odd) + whole * (2 * (r - odd) + across_whole)
+            s = c - back
+
+            @pl.when(whole == 0)
             def _():
                 tp_all(s).wait_recv()
 
-            @pl.when(i % 2 == 0)
+            @pl.when(whole == 1)
             def _():
                 half_copy(s, 2).wait_recv()
 
@@ -445,16 +462,6 @@
         pick[e] = jnp.where(chosen, 1.0, 0.0).astype(BF16)
         give[e] = jnp.where(chosen, gate[e : e + 1], 0.0).astype(BF16)
 
-    use(7)
-    use(8)
-    for n in range(CHUNKS):
-        hidden[:, cols(n)] = residual[:, cols(n)].astype(F32) + sum_rows(
-            n, row_in, a_row_send, a_row_recv
-        )
-    state = hidden[...]
-    mean_square = jnp.mean(state * state, axis=1, keepdims=True)
-    normed[core, chip] = (state * lax.rsqrt(mean_square + 1e-06) * gain[...].reshape(1, width)).astype(BF16)
-
     def normed_copy(n, d):
         block = normed.at[core, chip, :, cols(n)]
         return remote(block, block, n_send.at[0], n_recv.at[n], chip_at(d)[1])
@@ -473,8 +480,23 @@
         half_rows = normed.at[core]
         remote(half_rows, half_rows, n_sib_send.at[0], n_sib_recv.at[0], sibling).wait_send()
 
-    for n in range(CHUNKS):
+    def send_rows(n):
+        state = residual[:, cols(n)].astype(F32) + sum_rows(n, row_in, a_row_send, a_row_recv)
+        hidden[:, cols(n)] = state
+        normed[core, chip, :, cols(n)] = (state * gain[cols(n)].reshape(1, span)).astype(BF16)
         loop(1, n_chip, lambda d: normed_copy(n, d).start())
+
+    def square_sum(block, n):
+        plain = block.astype(F32) * (1.0 / gain[cols(n)].reshape(1, span))
+        return jnp.sum(plain * plain, axis=1, keepdims=True)
+
+    def norm_factor(total):
+        return lax.rsqrt(total * (1.0 / width) + 1e-06)
+
+    use(7)
+    use(8)
+    for n in range(LEAD):
+        send_rows(n)
     pending.append(normed_sent)
 
     def slot_copy(n, d, source, landing, send, recv):
@@ -493,7 +515,10 @@
 
     there = (slots_out, slots_in, x_send, x_recv)
     back = (back_out, back_in, y_send, y_recv)
+    group_squares = 0.0
     for n in range(CHUNKS):
+        if n + LEAD < CHUNKS:
+            send_rows(n + LEAD)
         normed_all(n).wait_recv()
         normed_sib(n).start()
         normed_sib(n).wait_recv()
@@ -502,13 +527,15 @@
         slots_out[:, :, cols(n)] = picked.reshape(n_ctx, slot_room, span)
         loop(1, n_ctx, lambda d: slot_copy(n, d, *there).start())
         slots_in[c, :, cols(n)] = slots_out[c, :, cols(n)]
+        group_squares = group_squares + square_sum(block, n)
     pending.append(functools.partial(slots_sent, *there))
 
     use(10)
     use(11)
     everyone = normed[...].reshape(group, width)
-    gate_part = dot_rows(everyone, shared_gate[...])
-    up_part = dot_rows(everyone, shared_up[...])
+    factor = norm_factor(group_squares)
+    gate_part = dot_rows(everyone, shared_gate[...]) * factor
+    up_part = dot_rows(everyone, shared_up[...]) * factor
     shared_hidden = (gate_part / (1.0 + jnp.exp(-gate_part)) * up_part).astype(BF16)
     use(12)
     for n in range(CHUNKS):
@@ -516,17 +543,21 @@
 
     use(13)
     use(14)
+    slot_squares = 0.0
     for n in range(CHUNKS):
         slot_wait(n, *there)
         items = slots_in[:, :, cols(n)].reshape(n_ctx * slot_room, span)
         product = dot(items, gate_up[cols(n), :])
+        slot_squares = slot_squares + square_sum(items, n)
         if n == 0:
             up_acc[...] = product
         else:
             up_acc[...] = up_acc[...] + product
     inner = down.shape[0]
-    gate_part = up_acc[:, :inner]
-    expert_hidden = (gate_part / (1.0 + jnp.exp(-gate_part)) * up_acc[:, inner:]).astype(BF16)
+    factor = norm_factor(slot_squares)
+    gate_part = up_acc[:, :inner] * factor
+    up_part = up_acc[:, inner:] * factor
+    expert_hidden = (gate_part / (1.0 + jnp.exp(-gate_part)) * up_part).astype(BF16)
     for n in range(CHUNKS):
         result = dot(expert_hidden, down[:, cols(n)]).astype(BF16)
         back_out[:, :, cols(n)] = result.reshape(n_ctx, slot_room, span)

time: 125 us -> 119 us (0.952)
  Pallas kernels: 121 us -> 115 us
    pallas_call x1, Pallas kernels: 121 us -> 115 us  [shards(): pl.pallas_call(layer_kernel, out_shape=jax.ShapeDtypeStruct((rows, width)...]
where the time goes in v3:
time: 119 us; the launch traced here: 117 us
  Pallas kernels  115 us (97%)
  local copies, waits for them, and re-layouts  1.59 us (1%)
    pallas_call x1, Pallas kernels, shards(): pl.pallas_call(layer_kernel, out_shape=jax.ShapeDtypeStruct((rows, width)...  115 us

profile of v3, /device:TPU:16, one launch (start us, length us, event | category | flops | bytes accessed | tf_op | source)
XLA Modules:
  0.0 117.0 jit_solution(15808268354652668998)
XLA Ops:
  0.0 115.4 %layer.1 = bf16[32,2560]{1,0:T(8,128)(2,1)} custom-call(bf16[512,768]{1,0:T(8,128)(2,1)} %queries_hbm.1, bf16[32,512]{1,0:T(8,128)(2,1)} %kv_latent_hbm.1, bf16[32,64]{1,0:T(8,128)(2,1)} %key_rope_hbm.1, bf16[512,512]{1,0:T(8,128)(2,1)} %w_key_hbm.1, bf16[512,512]{1,0:T(8,128)(2,1)} %w_value_hbm.1, bf16[512,2560]{1,0:T(8,128)(2,1)} %w_out_hbm.1, ...), custom_call_target="tpu_custom_call" | custom-call | flops 20000000000 | bytes 20000000 | tf_op jit(solution)/shard_map/layer/pallas_call | solution.py:678
  115.4 1.6 %copy.17 = bf16[32,2560]{1,0:T(8,128)(2,1)} copy(bf16[32,2560]{1,0:T(8,128)(2,1)} %layer.1) | data formatting | bytes 327680

commit v4 on v3

--- a/solution.py
+++ b/solution.py
@@ -19,6 +19,7 @@
 LOW = -1e30
 CHUNKS = 10
 LEAD = 3
+EARLY = 1
 
 
 def loop(first, end, body):
@@ -134,7 +135,7 @@
     half = n_chip * rows
     group = 2 * half
     span = width // CHUNKS
-    slot_room = slots_out.shape[1]
+    slot_room = slots_out.shape[2]
 
     def cols(n):
         return pl.ds(n * span, span)
@@ -248,9 +249,25 @@
         )
 
     odd = c % 2
-    later = (n_ctx - 1 - c) // 2
+    later = n_ctx - 1 - c
     earlier = c // 2
-    loop(0, later, lambda i: block_copy(c, 2 * (later - i) + 1 - 2 * odd).start())
+    passed = earlier + c // 4
+
+    def each_later(whole, body):
+        if whole:
+
+            @pl.when(odd == 0)
+            def _():
+                body(1)
+
+            for d in (6, 2):
+                pl.when(later >= d)(functools.partial(body, d))
+        else:
+            loop(0, later // 2, lambda i: body(2 * (later // 2 - i) + 1 - 2 * odd))
+            pl.when(later >= 4)(functools.partial(body, 4))
+
+    def passed_back(i):
+        return jnp.where(i <= earlier, 2 * i - 1 + 2 * odd, 4)
 
     def tp_copy(s, d):
         held = (chip + across(s)) % n_chip
@@ -267,6 +284,7 @@
         return remote(blocks, blocks, lat_tp_send.at[s], lat_tp_recv.at[s], sibling)
 
     loop(1, n_chip, lambda d: tp_copy(c, d).start())
+    each_later(False, lambda d: block_copy(c, d).start())
 
     use(4)
     q_all = queries[...].reshape(n_chip, 2, rows, queries.shape[1])
@@ -281,22 +299,17 @@
     acc_s[...] = jnp.zeros(acc_s.shape, F32)
 
     def pass_on(i):
-        s = c - 2 * i - 1 - 2 * odd
+        s = c - passed_back(i)
         block_copy(s, 1).wait_recv()
         loop(1, n_chip, lambda d: tp_copy(s, d).start())
 
-    loop(0, earlier, pass_on)
+    loop(1, passed + 1, pass_on)
 
     def lat_sent():
-        loop(0, later, lambda i: block_copy(c, 2 * (later - i) + 1 - 2 * odd).wait_send())
-        loop(0, later, lambda i: half_copy(c, 2 * (later - i)).wait_send())
-
-        @pl.when(odd == 0)
-        def _():
-            half_copy(c, 1).wait_send()
-
+        each_later(False, lambda d: block_copy(c, d).wait_send())
+        each_later(True, lambda d: half_copy(c, d).wait_send())
         tp_all(c).wait_send()
-        loop(0, earlier, lambda i: tp_all(c - 2 * i - 1 - 2 * odd).wait_send())
+        loop(1, passed + 1, lambda i: tp_all(c - passed_back(i)).wait_send())
         loop(0, c + 1, lambda i: sib_copy(c - i, core).wait_send())
 
     pending.append(lat_sent)
@@ -307,19 +320,24 @@
         i = lax.broadcasted_iota(jnp.int32, axis_shape, axis) + index
         return ((i & (half - 1)) // rows) * (2 * rows) + (i // half) * rows + (i & (rows - 1))
 
-    def attend(s, k, diagonal):
-        block = lat[s, k].reshape(half, lat.shape[4])
-        k_s[...] = dot(block[:, :latent], w_key[...]).astype(BF16)
-        v_s[...] = dot(block[:, :latent], w_value[...]).astype(BF16)
+    def attend(s, k=None):
+        diagonal = k is not None
+        block = lat[s, k] if diagonal else lat[s]
+        block = block.reshape(-1, lat.shape[4])
+        count = block.shape[0]
+        k_s[:count] = dot(block[:, :latent], w_key[...]).astype(BF16)
+        v_s[:count] = dot(block[:, :latent], w_value[...]).astype(BF16)
         rope = block[:, latent:]
-        ones = jnp.ones((half, VDIM), BF16)
+        ones = jnp.ones((count, VDIM), BF16)
+        if diagonal:
+            query_at = place(0, (group, 128), 0)
+            query_at = jnp.concatenate([query_at] * (count // 128), axis=1)
+            key_at = place(k * half, (8, count), 1)[:1]
         for h in range(heads):
-            keys = jnp.concatenate([k_s[:, h * NOPE : (h + 1) * NOPE], rope], axis=1)
-            values = jnp.concatenate([v_s[:, h * VDIM : (h + 1) * VDIM], ones], axis=1)
+            keys = jnp.concatenate([k_s[:count, h * NOPE : (h + 1) * NOPE], rope], axis=1)
+            values = jnp.concatenate([v_s[:count, h * VDIM : (h + 1) * VDIM], ones], axis=1)
             scores = dot_rows(q_s[h], keys)
             if diagonal:
-                query_at = place(0, (group, half), 0)
-                key_at = place(k * half, (group, half), 1)
                 scores = jnp.where(key_at <= query_at, scores, LOW)
             top_old = top_s[h]
             top_new = jnp.maximum(top_old, jnp.max(scores, axis=1, keepdims=True))
@@ -327,7 +345,7 @@
             weights = jnp.concatenate(
                 [
                     jnp.exp2((scores[:, j * 128 : (j + 1) * 128] - top_new) * scale).astype(BF16)
-                    for j in range(half // 128)
+                    for j in range(count // 128)
                 ],
                 axis=1,
             )
@@ -338,52 +356,61 @@
     def sib_copy(s, k):
         return remote(lat.at[s, k], lat.at[s, k], lat_sib_send.at[s], lat_sib_recv.at[s], sibling)
 
-    def key_step(q, diagonal):
-        if diagonal:
-            s = c
-            tp_all(s).wait_recv()
-
-            @pl.when(odd == 0)
-            def _():
-                half_copy(c, 1).start()
-
-            loop(0, later, lambda i: half_copy(c, 2 * (later - i)).start())
-        else:
-            whole = q // (earlier + 1)
-            r = jnp.maximum(q - earlier, 1)
-            across_whole = odd * (1 // r)
-            back = (1 - whole) * (2 * q - 1 + 2 * odd) + whole * (2 * (r - odd) + across_whole)
-            s = c - back
-
-            @pl.when(whole == 0)
-            def _():
-                tp_all(s).wait_recv()
-
-            @pl.when(whole == 1)
-            def _():
-                half_copy(s, 2).wait_recv()
-
-        sib_copy(s, core).start()
-
-        def half_step(j):
-            @pl.when(j == 1)
-            def _():
-                sib_copy(s, other).wait_recv()
-
-            attend(s, (core + j) % 2, diagonal)
-
-        loop(0, 2, half_step)
-
+    ahead = jnp.minimum(passed, EARLY)
+    halves = c - passed
+
+    def block_at(q):
+        whole = jnp.where(q <= ahead, 0, jnp.where(q <= ahead + halves, 1, 0))
+        r = q - ahead
+        half_back = jnp.where(r <= odd, 1, 4 * (r - odd) - 2)
+        i = jnp.where(q <= ahead, q, q - halves)
+        return c - jnp.where(whole == 1, half_back, passed_back(i)), whole
+
+    tp_all(c).wait_recv()
+    each_later(True, lambda d: half_copy(c, d).start())
+    sib_copy(c, core).start()
     use(5)
     use(6)
-    key_step(0, True)
+
+    def own_step(j):
+        @pl.when(j == 1)
+        def _():
+            sib_copy(c, other).wait_recv()
+
+        attend(c, (core + j) % 2)
+
+    loop(0, jnp.minimum(2, c + 2), own_step)
     loads[9].start()
-    loop(1, c + 1, lambda i: key_step(i, False))
+
+    def key_step(q):
+        s, whole = block_at(q)
+
+        @pl.when((q <= c) & (whole == 0))
+        def _():
+            tp_all(s).wait_recv()
+
+        @pl.when((q <= c) & (whole == 1))
+        def _():
+            half_copy(s, 2).wait_recv()
+
+        @pl.when(q <= c)
+        def _():
+            sib_copy(s, core).start()
+
+        @pl.when(q > 1)
+        def _():
+            attend(block_at(q - 1)[0])
+
+        @pl.when(q <= c)
+        def _():
+            sib_copy(s, other).wait_recv()
+
+    loop(1, c + 2, key_step)
 
     def sib_part(n, buffer, landing, send, recv):
         return remote(
-            buffer.at[other, :, :, cols(n)],
-            landing.at[:, :, cols(n)],
+            buffer.at[n, other],
+            landing.at[n],
             send.at[0],
             recv.at[n],
             sibling,
@@ -392,8 +419,8 @@
     def row_part(n, d, buffer, landing, send, recv):
         j, device = chip_at(d)
         return remote(
-            buffer.at[core, j, :, cols(n)],
-            landing.at[chip, :, cols(n)],
+            buffer.at[n, core, j],
+            landing.at[n, chip],
             send.at[0],
             recv.at[n],
             device,
@@ -402,25 +429,25 @@
     def pass_rows(n, buffer, from_sibling, landing, sib_send, sib_recv, send, recv):
         sib_part(n, buffer, from_sibling, sib_send, sib_recv).wait_recv()
         summed = (
-            buffer[core, :, :, cols(n)].astype(F32) + from_sibling[:, :, cols(n)].astype(F32)
+            buffer[n, core].astype(F32) + from_sibling[n].astype(F32)
         ).astype(BF16)
-        buffer[core, :, :, cols(n)] = summed
-        landing[chip, :, cols(n)] = buffer[core, chip, :, cols(n)]
+        buffer[n, core] = summed
+        landing[n, chip] = buffer[n, core, chip]
         loop(1, n_chip, lambda d: row_part(n, d, buffer, landing, send, recv).start())
 
     def rows_sent(buffer, from_sibling, landing, sib_send, sib_recv, send, recv):
         remote(
-            buffer.at[other], from_sibling, sib_send.at[0], sib_recv.at[0], sibling
+            buffer.at[:, other], from_sibling, sib_send.at[0], sib_recv.at[0], sibling
         ).wait_send()
         others = pl.ds(0, n_chip - 1)
         remote(
-            buffer.at[core, others], landing.at[others], send.at[0], recv.at[0], sibling
+            buffer.at[:, core, others], landing.at[:, others], send.at[0], recv.at[0], sibling
         ).wait_send()
 
     def sum_rows(n, landing, send, recv):
-        blocks = landing.at[pl.ds(0, n_chip - 1), :, cols(n)]
+        blocks = landing.at[n, pl.ds(0, n_chip - 1)]
         remote(blocks, blocks, send.at[0], recv.at[n], sibling).wait_recv()
-        return jnp.sum(landing[:, :, cols(n)].astype(F32), axis=0)
+        return jnp.sum(landing[n].astype(F32), axis=0)
 
     attention = jnp.concatenate(
         [(acc_s[h, :, :VDIM] / acc_s[h, :, VDIM:]).astype(BF16) for h in range(heads)], axis=1
@@ -428,7 +455,7 @@
     use(9)
     first = (part, sib_in, row_in, a_sib_send, a_sib_recv, a_row_send, a_row_recv)
     for n in range(CHUNKS):
-        part[:, :, :, cols(n)] = (
+        part[n] = (
             dot(attention, w_out[:, cols(n)]).astype(BF16).reshape(2, n_chip, rows, span)
         )
         sib_part(n, part, sib_in, a_sib_send, a_sib_recv).start()
@@ -463,27 +490,27 @@
         give[e] = jnp.where(chosen, gate[e : e + 1], 0.0).astype(BF16)
 
     def normed_copy(n, d):
-        block = normed.at[core, chip, :, cols(n)]
+        block = normed.at[n, core, chip]
         return remote(block, block, n_send.at[0], n_recv.at[n], chip_at(d)[1])
 
     def normed_all(n):
-        blocks = normed.at[core, pl.ds(0, n_chip - 1), :, cols(n)]
+        blocks = normed.at[n, core, pl.ds(0, n_chip - 1)]
         return remote(blocks, blocks, n_send.at[0], n_recv.at[n], sibling)
 
     def normed_sib(n):
-        half_rows = normed.at[core, :, :, cols(n)]
+        half_rows = normed.at[n, core]
         return remote(half_rows, half_rows, n_sib_send.at[0], n_sib_recv.at[n], sibling)
 
     def normed_sent():
-        blocks = normed.at[core, pl.ds(0, n_chip - 1)]
+        blocks = normed.at[:, core, pl.ds(0, n_chip - 1)]
         remote(blocks, blocks, n_send.at[0], n_recv.at[0], sibling).wait_send()
-        half_rows = normed.at[core]
+        half_rows = normed.at[:, core]
         remote(half_rows, half_rows, n_sib_send.at[0], n_sib_recv.at[0], sibling).wait_send()
 
     def send_rows(n):
         state = residual[:, cols(n)].astype(F32) + sum_rows(n, row_in, a_row_send, a_row_recv)
         hidden[:, cols(n)] = state
-        normed[core, chip, :, cols(n)] = (state * gain[cols(n)].reshape(1, span)).astype(BF16)
+        normed[n, core, chip] = (state * gain[cols(n)].reshape(1, span)).astype(BF16)
         loop(1, n_chip, lambda d: normed_copy(n, d).start())
 
     def square_sum(block, n):
@@ -502,40 +529,50 @@
     def slot_copy(n, d, source, landing, send, recv):
         j, device = ctx_at(d)
         return remote(
-            source.at[j, :, cols(n)], landing.at[c, :, cols(n)], send.at[0], recv.at[n], device
+            source.at[n, j], landing.at[n, c], send.at[0], recv.at[n], device
         )
 
     def slot_wait(n, source, landing, send, recv):
-        blocks = landing.at[pl.ds(0, n_ctx - 1), :, cols(n)]
+        blocks = landing.at[n, pl.ds(0, n_ctx - 1)]
         remote(blocks, blocks, send.at[0], recv.at[n], sibling).wait_recv()
 
     def slots_sent(source, landing, send, recv):
-        blocks = source.at[pl.ds(0, n_ctx - 1)]
+        blocks = source.at[:, pl.ds(0, n_ctx - 1)]
         remote(blocks, blocks, send.at[0], recv.at[0], sibling).wait_send()
 
     there = (slots_out, slots_in, x_send, x_recv)
     back = (back_out, back_in, y_send, y_recv)
-    group_squares = 0.0
+    def dispatch(n):
+        normed_sib(n).wait_recv()
+        block = normed[n].reshape(group, span)
+        picked = dot(pick[...].reshape(n_ctx * slot_room, group), block).astype(BF16)
+        slots_out[n] = picked.reshape(n_ctx, slot_room, span)
+        loop(1, n_ctx, lambda d: slot_copy(n, d, *there).start())
+        slots_in[n, c] = slots_out[n, c]
+
     for n in range(CHUNKS):
         if n + LEAD < CHUNKS:
             send_rows(n + LEAD)
         normed_all(n).wait_recv()
         normed_sib(n).start()
-        normed_sib(n).wait_recv()
-        block = normed[:, :, :, cols(n)].reshape(group, span)
-        picked = dot(pick[...].reshape(n_ctx * slot_room, group), block).astype(BF16)
-        slots_out[:, :, cols(n)] = picked.reshape(n_ctx, slot_room, span)
-        loop(1, n_ctx, lambda d: slot_copy(n, d, *there).start())
-        slots_in[c, :, cols(n)] = slots_out[c, :, cols(n)]
-        group_squares = group_squares + square_sum(block, n)
+        if n > 0:
+            dispatch(n - 1)
+    dispatch(CHUNKS - 1)
     pending.append(functools.partial(slots_sent, *there))
 
     use(10)
     use(11)
-    everyone = normed[...].reshape(group, width)
+    group_squares = 0.0
+    gate_sum = 0.0
+    up_sum = 0.0
+    for n in range(CHUNKS):
+        block = normed[n].reshape(group, span)
+        group_squares = group_squares + square_sum(block, n)
+        gate_sum = gate_sum + dot_rows(block, shared_gate[:, cols(n)])
+        up_sum = up_sum + dot_rows(block, shared_up[:, cols(n)])
     factor = norm_factor(group_squares)
-    gate_part = dot_rows(everyone, shared_gate[...]) * factor
-    up_part = dot_rows(everyone, shared_up[...]) * factor
+    gate_part = gate_sum * factor
+    up_part = up_sum * factor
     shared_hidden = (gate_part / (1.0 + jnp.exp(-gate_part)) * up_part).astype(BF16)
     use(12)
     for n in range(CHUNKS):
@@ -546,7 +583,7 @@
     slot_squares = 0.0
     for n in range(CHUNKS):
         slot_wait(n, *there)
-        items = slots_in[:, :, cols(n)].reshape(n_ctx * slot_room, span)
+        items = slots_in[n].reshape(n_ctx * slot_room, span)
         product = dot(items, gate_up[cols(n), :])
         slot_squares = slot_squares + square_sum(items, n)
         if n == 0:
@@ -560,18 +597,18 @@
     expert_hidden = (gate_part / (1.0 + jnp.exp(-gate_part)) * up_part).astype(BF16)
     for n in range(CHUNKS):
         result = dot(expert_hidden, down[:, cols(n)]).astype(BF16)
-        back_out[:, :, cols(n)] = result.reshape(n_ctx, slot_room, span)
+        back_out[n] = result.reshape(n_ctx, slot_room, span)
         loop(1, n_ctx, lambda d: slot_copy(n, d, *back).start())
-        back_in[c, :, cols(n)] = back_out[c, :, cols(n)]
+        back_in[n, c] = back_out[n, c]
     pending.append(functools.partial(slots_sent, *back))
 
     give_rows = give[...].reshape(n_ctx * slot_room, group).astype(F32).T.astype(BF16)
     second = (part2, sib_in2, row_in2, b_sib_send, b_sib_recv, b_row_send, b_row_recv)
     for n in range(CHUNKS):
         slot_wait(n, *back)
-        returned = back_in[:, :, cols(n)].reshape(n_ctx * slot_room, span)
+        returned = back_in[n].reshape(n_ctx * slot_room, span)
         both = shared_acc[:, cols(n)] + dot(give_rows, returned)
-        part2[:, :, :, cols(n)] = both.astype(BF16).reshape(2, n_chip, rows, span)
+        part2[n] = both.astype(BF16).reshape(2, n_chip, rows, span)
         sib_part(n, part2, sib_in2, b_sib_send, b_sib_recv).start()
         if n > 0:
             pass_rows(n - 1, *second)
@@ -580,7 +617,7 @@
     for n in range(CHUNKS):
         out_ref[:, cols(n)] = (
             hidden[:, cols(n)] + sum_rows(n, row_in2, b_row_send, b_row_recv)
-        ).astype(BF16)
+        )
 
     finish()
 
@@ -630,8 +667,8 @@
         dma((15,)),
         pltpu.VMEM((n_ctx, 2, n_chip, rows, latent + 128), BF16),
         pltpu.VMEM((heads, group, 2 * NOPE), BF16),
-        pltpu.VMEM((group // 2, heads * NOPE), BF16),
-        pltpu.VMEM((group // 2, heads * VDIM), BF16),
+        pltpu.VMEM((group, heads * NOPE), BF16),
+        pltpu.VMEM((group, heads * VDIM), BF16),
         pltpu.VMEM((heads, group, 128), F32),
         pltpu.VMEM((heads, group, 2 * VDIM), F32),
         dma((n_ctx,)),
@@ -640,34 +677,34 @@
         dma((n_ctx,)),
         dma((n_ctx,)),
         dma((n_ctx,)),
-        pltpu.VMEM((2, n_chip, rows, width), BF16),
-        pltpu.VMEM((n_chip, rows, width), BF16),
-        pltpu.VMEM((n_chip, rows, width), BF16),
+        pltpu.VMEM((CHUNKS, 2, n_chip, rows, width // CHUNKS), BF16),
+        pltpu.VMEM((CHUNKS, n_chip, rows, width // CHUNKS), BF16),
+        pltpu.VMEM((CHUNKS, n_chip, rows, width // CHUNKS), BF16),
         dma((1,)),
         dma((CHUNKS,)),
         dma((1,)),
         dma((CHUNKS,)),
         pltpu.VMEM((rows, width), F32),
-        pltpu.VMEM((2, n_chip, rows, width), BF16),
+        pltpu.VMEM((CHUNKS, 2, n_chip, rows, width // CHUNKS), BF16),
         dma((1,)),
         dma((CHUNKS,)),
         dma((1,)),
         dma((CHUNKS,)),
         pltpu.VMEM((n_ctx, slot_room, group), BF16),
         pltpu.VMEM((n_ctx, slot_room, group), BF16),
-        pltpu.VMEM((n_ctx, slot_room, width), BF16),
-        pltpu.VMEM((n_ctx, slot_room, width), BF16),
+        pltpu.VMEM((CHUNKS, n_ctx, slot_room, width // CHUNKS), BF16),
+        pltpu.VMEM((CHUNKS, n_ctx, slot_room, width // CHUNKS), BF16),
         pltpu.VMEM((n_ctx * slot_room, expert_gate_up.shape[2]), F32),
         dma((1,)),
         dma((CHUNKS,)),
-        pltpu.VMEM((n_ctx, slot_room, width), BF16),
-        pltpu.VMEM((n_ctx, slot_room, width), BF16),
+        pltpu.VMEM((CHUNKS, n_ctx, slot_room, width // CHUNKS), BF16),
+        pltpu.VMEM((CHUNKS, n_ctx, slot_room, width // CHUNKS), BF16),
         dma((1,)),
         dma((CHUNKS,)),
         pltpu.VMEM((group, width), F32),
-        pltpu.VMEM((2, n_chip, rows, width), BF16),
-        pltpu.VMEM((n_chip, rows, width), BF16),
-        pltpu.VMEM((n_chip, rows, width), BF16),
+        pltpu.VMEM((CHUNKS, 2, n_chip, rows, width // CHUNKS), BF16),
+        pltpu.VMEM((CHUNKS, n_chip, rows, width // CHUNKS), BF16),
+        pltpu.VMEM((CHUNKS, n_chip, rows, width // CHUNKS), BF16),
         dma((1,)),
         dma((CHUNKS,)),
         dma((1,)),
@@ -677,7 +714,7 @@
     hbm = pl.BlockSpec(memory_space=pl.ANY)
     return pl.pallas_call(
         layer_kernel,
-        out_shape=jax.ShapeDtypeStruct((rows, width), BF16),
+        out_shape=jax.ShapeDtypeStruct((rows, width), F32),
         in_specs=[hbm] * 15,
         out_specs=vmem,
         scratch_shapes=scratch,
@@ -704,7 +741,7 @@
         expert_down,
         expert_ids.T,
         gate_weights.T,
-    )
+    ).astype(BF16)
 
 
 def solution(mesh):

time: 119 us -> 118 us (level)
  other arithmetic: 0 us -> 1.66 us
  local copies, waits for them, and re-layouts: 1.59 us -> 0 us
    convert_element_type x0 -> x1, other arithmetic: none -> 1.66 us  [shards(): return pl.pallas_call(layer_kernel, out_shape=jax.ShapeDtypeStruct((rows,...]
    unnamed x1 -> x0, local copies, waits for them, and re-layouts: 1.59 us -> none
where the time goes in v4:
time: 118 us; the launch traced here: 117 us
  Pallas kernels  115 us (97%)
  other arithmetic  1.66 us (1%)
    pallas_call x1, Pallas kernels, shards(): pl.pallas_call(layer_kernel, out_shape=jax.ShapeDtypeStruct((rows, width)...  115 us

profile of v4, /device:TPU:16, one launch (start us, length us, event | category | flops | bytes accessed | tf_op | source)
XLA Modules:
  0.0 116.5 jit_solution(15603740341461524596)
XLA Ops:
  0.0 114.9 %layer.1 = f32[32,2560]{1,0:T(8,128)} custom-call(bf16[512,768]{1,0:T(8,128)(2,1)} %queries_hbm.1, bf16[32,512]{1,0:T(8,128)(2,1)} %kv_latent_hbm.1, bf16[32,64]{1,0:T(8,128)(2,1)} %key_rope_hbm.1, bf16[512,512]{1,0:T(8,128)(2,1)} %w_key_hbm.1, bf16[512,512]{1,0:T(8,128)(2,1)} %w_value_hbm.1, bf16[512,2560]{1,0:T(8,128)(2,1)} %w_out_hbm.1, ...), custom_call_target="tpu_custom_call" | custom-call | flops 20000000000 | bytes 20000000 | tf_op jit(solution)/shard_map/layer/pallas_call | solution.py:715
  114.9 1.7 %convert_element_type.3 = bf16[32,2560]{1,0:T(8,128)(2,1)} convert(f32[32,2560]{1,0:T(8,128)} %layer.1) | non-fusion elementwise | flops 81920 | bytes 491520 | tf_op jit(solution)/shard_map/convert_element_type | solution.py:744

commit v5 on v4

--- a/solution.py
+++ b/solution.py
@@ -112,7 +112,6 @@
     back_in,
     y_send,
     y_recv,
-    shared_acc,
     part2,
     sib_in2,
     row_in2,
@@ -560,24 +559,6 @@
     dispatch(CHUNKS - 1)
     pending.append(functools.partial(slots_sent, *there))
 
-    use(10)
-    use(11)
-    group_squares = 0.0
-    gate_sum = 0.0
-    up_sum = 0.0
-    for n in range(CHUNKS):
-        block = normed[n].reshape(group, span)
-        group_squares = group_squares + square_sum(block, n)
-        gate_sum = gate_sum + dot_rows(block, shared_gate[:, cols(n)])
-        up_sum = up_sum + dot_rows(block, shared_up[:, cols(n)])
-    factor = norm_factor(group_squares)
-    gate_part = gate_sum * factor
-    up_part = up_sum * factor
-    shared_hidden = (gate_part / (1.0 + jnp.exp(-gate_part)) * up_part).astype(BF16)
-    use(12)
-    for n in range(CHUNKS):
-        shared_acc[:, cols(n)] = dot(shared_hidden, shared_down[:, cols(n)])
-
     use(13)
     use(14)
     slot_squares = 0.0
@@ -602,12 +583,28 @@
         back_in[n, c] = back_out[n, c]
     pending.append(functools.partial(slots_sent, *back))
 
+    use(10)
+    use(11)
+    group_squares = 0.0
+    gate_sum = 0.0
+    up_sum = 0.0
+    for n in range(CHUNKS):
+        block = normed[n].reshape(group, span)
+        group_squares = group_squares + square_sum(block, n)
+        gate_sum = gate_sum + dot_rows(block, shared_gate[:, cols(n)])
+        up_sum = up_sum + dot_rows(block, shared_up[:, cols(n)])
+    factor = norm_factor(group_squares)
+    gate_part = gate_sum * factor
+    up_part = up_sum * factor
+    shared_hidden = (gate_part / (1.0 + jnp.exp(-gate_part)) * up_part).astype(BF16)
+    use(12)
+
     give_rows = give[...].reshape(n_ctx * slot_room, group).astype(F32).T.astype(BF16)
     second = (part2, sib_in2, row_in2, b_sib_send, b_sib_recv, b_row_send, b_row_recv)
     for n in range(CHUNKS):
         slot_wait(n, *back)
         returned = back_in[n].reshape(n_ctx * slot_room, span)
-        both = shared_acc[:, cols(n)] + dot(give_rows, returned)
+        both = dot(shared_hidden, shared_down[:, cols(n)]) + dot(give_rows, returned)
         part2[n] = both.astype(BF16).reshape(2, n_chip, rows, span)
         sib_part(n, part2, sib_in2, b_sib_send, b_sib_recv).start()
         if n > 0:
@@ -701,7 +698,6 @@
         pltpu.VMEM((CHUNKS, n_ctx, slot_room, width // CHUNKS), BF16),
         dma((1,)),
         dma((CHUNKS,)),
-        pltpu.VMEM((group, width), F32),
         pltpu.VMEM((CHUNKS, 2, n_chip, rows, width // CHUNKS), BF16),
         pltpu.VMEM((CHUNKS, n_chip, rows, width // CHUNKS), BF16),
         pltpu.VMEM((CHUNKS, n_chip, rows, width // CHUNKS), BF16),

time: 118 us -> 118 us (level)
  no operation moved by 1% of the time
where the time goes in v5:
time: 118 us; the launch traced here: 117 us
  Pallas kernels  115 us (97%)
  other arithmetic  1.66 us (1%)
    pallas_call x1, Pallas kernels, shards(): pl.pallas_call(layer_kernel, out_shape=jax.ShapeDtypeStruct((rows, width)...  115 us

profile of v5, /device:TPU:16, one launch (start us, length us, event | category | flops | bytes accessed | tf_op | source)
XLA Modules:
  0.0 116.7 jit_solution(11517087195963271102)
XLA Ops:
  0.0 115.0 %layer.1 = f32[32,2560]{1,0:T(8,128)} custom-call(bf16[512,768]{1,0:T(8,128)(2,1)} %queries_hbm.1, bf16[32,512]{1,0:T(8,128)(2,1)} %kv_latent_hbm.1, bf16[32,64]{1,0:T(8,128)(2,1)} %key_rope_hbm.1, bf16[512,512]{1,0:T(8,128)(2,1)} %w_key_hbm.1, bf16[512,512]{1,0:T(8,128)(2,1)} %w_value_hbm.1, bf16[512,2560]{1,0:T(8,128)(2,1)} %w_out_hbm.1, ...), custom_call_target="tpu_custom_call" | custom-call | flops 20000000000 | bytes 20000000 | tf_op jit(solution)/shard_map/layer/pallas_call | solution.py:711
  115.0 1.7 %convert_element_type.3 = bf16[32,2560]{1,0:T(8,128)(2,1)} convert(f32[32,2560]{1,0:T(8,128)} %layer.1) | non-fusion elementwise | flops 81920 | bytes 491520 | tf_op jit(solution)/shard_map/convert_element_type | solution.py:740
